TPU v7x, 512 devices: a whole 4x8x8 slice. The times are simulated.
512 devices in a mesh: dp: 2 (over core), ctx: 32 (over z, x), tp: 8 (over y).
Axes of the slice: x: 4, y: 8, z: 8, core: 2. Of those that a mesh axis runs over, the one named last changes fastest.
Arguments:
- query_rows: bfloat16 [2, 4096, 12288], P('dp', 'ctx', 'tp'), may hold values from -100 to 100
- key_rows: bfloat16 [2, 4096, 1024], P('dp', 'ctx', 'tp'), may hold values from -4 to 4
- value_matrix: bfloat16 [2, 4096, 1024], P('dp', 'ctx', 'tp'), may hold values from -6 to 6
- attention_result: bfloat16 [2, 4096, 12288], P('dp', 'ctx', 'tp'), may hold values from -6 to 6
- loss_output_gradient: bfloat16 [2, 4096, 12288], P('dp', 'ctx', 'tp'), may hold values from -6 to 6
- response_index: int32 [2, 4096], P('dp', 'ctx'), may hold values from 0 to 3, never falling along the last dimension, each value on 1 to 2048 neighbouring positions
- kv_weight: bfloat16 [12288, 2048], P(('dp', 'ctx'), 'tp'), may hold values from -0.0546875 to 0.0546875
Outputs:
- query_grad: bfloat16 [2, 4096, 12288], P('dp', 'ctx', 'tp')
- key_grad: bfloat16 [2, 4096, 1024], P('dp', 'ctx', 'tp')
- value_grad: bfloat16 [2, 4096, 1024], P('dp', 'ctx', 'tp')
- input_grad: bfloat16 [2, 4096, 12288], P('dp', ('ctx', 'tp'))
Inputs may be any that keep to these rules, and one draw needn't show every extreme that they name: `response_index`: in each row the numbers never fall; each response holds 1 to 2048 consecutive tokens and one holds exactly 2048.
All inputs are finite; a program needn't handle non-finite values.
Results may differ from a plain program's by a relative error of at most 0.018.
Values may be sent and summed in bfloat16 or wider, within the bound.
A program may use at most 64 MiB of HBM per device.

v0:
```python
import jax
import jax.numpy as jnp
from jax import lax
from jax.sharding import PartitionSpec as P

HEAD_SIZE = 128


def from_behind(value, axis, by):
    length = lax.axis_size(axis)
    pairs = [(i, i + by) for i in range(length) if 0 <= i + by < length]
    return lax.ppermute(value, axis, pairs)


def rotation(positions, width):
    half = width // 2
    inverse = jnp.exp(-jnp.log(1000000.0) * (2.0 * jnp.arange(half, dtype=jnp.float32) / width))
    angle = positions[:, None] * inverse[None, :]
    angle = jnp.concatenate([angle, angle], axis=-1)
    return (jnp.cos(angle), jnp.sin(angle))


def unrotate(grad, cosine, sine):
    half = grad.shape[-1] // 2
    turned = jnp.concatenate([-grad[..., half:], grad[..., :half]], axis=-1)
    return grad * cosine - turned * sine


def local(
    query_rows,
    key_rows,
    value_matrix,
    attention_result,
    loss_output_gradient,
    response_index,
    kv_weight,
):
    tok = response_index.shape[1]
    group = query_rows.shape[-1] // HEAD_SIZE
    scale = HEAD_SIZE ** (-0.5)
    query_matrix = query_rows[0].reshape(tok, group, HEAD_SIZE)
    grads_out = loss_output_gradient[0].reshape(tok, group, HEAD_SIZE)
    outputs = attention_result[0].reshape(tok, group, HEAD_SIZE)
    delta = jnp.transpose(
        jnp.sum(grads_out.astype(jnp.float32) * outputs.astype(jnp.float32), axis=-1)
    )
    own_kv = jnp.concatenate([key_rows[0], value_matrix[0]], axis=-1)
    own_seg = response_index[0]
    seg_label = (own_seg + 1).astype(jnp.bfloat16)
    width = lax.axis_size("ctx")
    reach = min(16, width // 2)
    place = lax.axis_index("ctx")

    def carry_on(step, state):
        moving, labels, stack, stack_labels = state
        moving, labels = from_behind((moving, labels), "ctx", 1)
        stack = lax.dynamic_update_index_in_dim(stack, moving, step, 0)
        stack_labels = lax.dynamic_update_index_in_dim(stack_labels, labels, step, 0)
        return (moving, labels, stack, stack_labels)

    start_state = (
        own_kv,
        seg_label,
        jnp.zeros((reach, tok, 2 * HEAD_SIZE), jnp.bfloat16),
        jnp.zeros((reach, tok), jnp.bfloat16),
    )
    _, _, far_kv, far_label = lax.fori_loop(0, reach, carry_on, start_state)
    blocks = reach // 4
    far_keys = far_kv.reshape(blocks, 4 * tok, 2 * HEAD_SIZE)
    far_labels = far_label.reshape(blocks, 4 * tok)
    index_local = jnp.arange(tok)
    own_allowed = (own_seg[:, None] == own_seg[None, :]) & (
        index_local[:, None] >= index_local[None, :]
    )

    def scores_of(block_kv, allowed):
        scores = (
            jnp.einsum(
                "qgd,kd->gqk",
                query_matrix,
                block_kv[:, :HEAD_SIZE],
                preferred_element_type=jnp.float32,
            )
            * scale
        )
        return jnp.where(allowed[None], scores, -jnp.inf)

    first = scores_of(own_kv, own_allowed)
    top = jnp.max(first, axis=-1)
    total = jnp.sum(jnp.exp(first - top[..., None]), axis=-1)

    def gather_stats(state, pieces):
        top, total = state
        block_kv, labels = pieces
        scores = scores_of(block_kv, seg_label[:, None] == labels[None, :])
        new_top = jnp.maximum(top, jnp.max(scores, axis=-1))
        total = total * jnp.exp(top - new_top) + jnp.sum(
            jnp.exp(scores - new_top[..., None]), axis=-1
        )
        return ((new_top, total), None)

    (top, total), _ = lax.scan(gather_stats, (top, total), (far_keys, far_labels))
    lse = top + jnp.log(total)

    def block_grads(block_kv, allowed):
        prob = jnp.exp(scores_of(block_kv, allowed) - lse[..., None])
        prob_b = prob.astype(jnp.bfloat16)
        keys = block_kv[:, :HEAD_SIZE]
        values = block_kv[:, HEAD_SIZE:]
        value_part = jnp.einsum(
            "gqk,qgd->kd", prob_b, grads_out, preferred_element_type=jnp.float32
        )
        dprob = jnp.einsum("qgd,kd->gqk", grads_out, values, preferred_element_type=jnp.float32)
        dscore = (prob * (dprob - delta[:, :, None])).astype(jnp.bfloat16)
        query_part = jnp.einsum("gqk,kd->qgd", dscore, keys, preferred_element_type=jnp.float32)
        key_part = (
            jnp.einsum("gqk,qgd->kd", dscore, query_matrix, preferred_element_type=jnp.float32)
            * scale
        )
        return (query_part, jnp.concatenate([key_part, value_part], axis=-1))

    query_own, own_part = block_grads(own_kv, own_allowed)

    def far_step(query_sum, pieces):
        block_kv, labels = pieces
        query_part, kv_part = block_grads(block_kv, seg_label[:, None] == labels[None, :])
        return (query_sum + query_part, kv_part)

    query_sum, far_parts = lax.scan(far_step, query_own, (far_keys, far_labels))
    far_parts = far_parts.reshape(reach, tok, 2 * HEAD_SIZE)

    def send_back(step, acc):
        addend = lax.dynamic_index_in_dim(far_parts, reach - 1 - step, 0, keepdims=False)
        return from_behind(acc + addend, "ctx", -1)

    arrived = lax.fori_loop(0, reach, send_back, jnp.zeros((tok, 2 * HEAD_SIZE), jnp.float32))
    kv_total = own_part + arrived
    key_sum = kv_total[:, :HEAD_SIZE]
    value_half = kv_total[:, HEAD_SIZE:].astype(jnp.bfloat16)
    query_grad = (query_sum * scale).astype(jnp.bfloat16).reshape(1, tok, group * HEAD_SIZE)
    key_grad = key_sum.astype(jnp.bfloat16).reshape(1, tok, HEAD_SIZE)
    value_grad = value_half.reshape(1, tok, HEAD_SIZE)
    positions = (place * tok + jnp.arange(tok)).astype(jnp.float32)
    cosine, sine = rotation(positions, HEAD_SIZE)
    grad_rows = jnp.concatenate(
        [unrotate(key_sum, cosine, sine).astype(jnp.bfloat16), value_half], axis=-1
    )
    full_weight = lax.all_gather(kv_weight, ("dp", "ctx"), axis=0, tiled=True)
    input_part = lax.psum_scatter(
        lax.dot_general(
            grad_rows, full_weight, (((1,), (1,)), ((), ())), preferred_element_type=jnp.float32
        ).astype(jnp.bfloat16),
        "tp",
        scatter_dimension=0,
        tiled=True,
    )
    input_grad = input_part[None]
    return (query_grad, key_grad, value_grad, input_grad)


def solution(mesh):
    in_specs = (
        P("dp", "ctx", "tp"),
        P("dp", "ctx", "tp"),
        P("dp", "ctx", "tp"),
        P("dp", "ctx", "tp"),
        P("dp", "ctx", "tp"),
        P("dp", "ctx"),
        P(("dp", "ctx"), "tp"),
    )
    out_specs = (
        P("dp", "ctx", "tp"),
        P("dp", "ctx", "tp"),
        P("dp", "ctx", "tp"),
        P("dp", ("ctx", "tp"), None),
    )
    return jax.shard_map(local, mesh=mesh, in_specs=in_specs, out_specs=out_specs, check_vma=False)
```

profile of v0, /device:TPU:56, one launch (start us, length us, event | category | flops | bytes accessed | tf_op | source)
XLA Modules:
  0.0 486.5 jit_solution(2192604877038278078)
XLA Ops:
  12.8 168.6 %while.58 = (s32[]{:T(128)}, bf16[128,256]{1,0:T(8,128)(2,1)S(1)}, bf16[128]{0:T(256)(128)(2,1)S(1)}, bf16[16,128,256]{2,1,0:T(8,128)(2,1)}, bf16[16,128]{1,0:T(8,128)(2,1)S(1)}, /*index=5*/s32[]{:T(128)}, s32[]{:T(128)}) while((s32[]{:T(128)}, bf16[128,256]{1,0:T(8,128)(2,1)S(1)}, bf16[128]{0:T(256)(128)(2,1)S(1)}, ...), condition=%wide.region_3.4_spmd, body=%wide.region_2.3_spmd.sunk | while | flops 2 | bytes 526509 | solution.py:67
  35.0 5.5 %collective-permute-start.1 = (bf16[128]{0:T(256)(128)(2,1)S(1)}, bf16[128]{0:T(256)(128)(2,1)S(1)}, u32[]{:S(2)}, u32[]{:S(2)}) collective-permute-start(bf16[128]{0:T(256)(128)(2,1)S(1)} %get-tuple-element.552), channel_id=1, source_target_pairs={{0,8},{8,16},{16,24},{24,32},{32,40},{40,48},{48,56},{56,64},{64,7... | collective-permute-start | bytes 776 | tf_op jit(solution)/shard_map/while/body/eval_jaxpr/ppermute | solution.py:12
  162.9 5.2 %collective-permute-start.1 = (bf16[128]{0:T(256)(128)(2,1)S(1)}, bf16[128]{0:T(256)(128)(2,1)S(1)}, u32[]{:S(2)}, u32[]{:S(2)}) collective-permute-start(bf16[128]{0:T(256)(128)(2,1)S(1)} %get-tuple-element.552), channel_id=1, source_target_pairs={{0,8},{8,16},{16,24},{24,32},{32,40},{40,48},{48,56},{56,64},{64,7... | collective-permute-start | bytes 776 | tf_op jit(solution)/shard_map/while/body/eval_jaxpr/ppermute | solution.py:12
  181.6 9.8 %while.59 = (s32[]{:T(128)}, f32[12,128]{1,0:T(8,128)S(1)}, f32[12,128]{1,0:T(8,128)S(1)}, bf16[128]{0:T(256)(128)(2,1)S(1)}, bf16[4,512]{1,0:T(4,128)(2,1)S(1)}...) while((s32[]{:T(128)}, f32[12,128]{1,0:T(8,128)S(1)}, ...), condition=%wide.region_7.8_spmd, body=%wide.region_4.7_spmd.sunk | while | flops 206900224 | bytes 7619933 | solution.py:102
  193.9 32.2 %while.60 = (s32[]{:T(128)}, f32[128,12,128]{0,2,1:T(8,128)}, f32[4,512,256]{2,1,0:T(8,128)}, bf16[4,512,256]{2,1,0:T(8,128)(2,1)}, bf16[128]{0:T(256)(128)(2,1)...) while((s32[]{:T(128)}, f32[128,12,128]{0,2,1:T(8,128)}, ...), condition=%wide.region_10.11_spmd, body=%wide.region_9.10_spmd.sunk | while | flops 1014956032 | bytes 25257900 | solution.py:129
  226.2 155.5 %while.61 = (s32[]{:T(128)}, f32[128,256]{1,0:T(8,128)S(1)}, f32[16,128,256]{2,1,0:T(8,128)}, s32[]{:T(128)}, s32[]{:T(128)}, /*index=5*/s32[]{:T(128)}, s32[]{:T(128)}) while((s32[]{:T(128)}, f32[128,256]{1,0:T(8,128)S(1)}, f32[16,128,256]{2,1,0:T(8,128)}, s32[]{:T(128)}, s32[]{:T(128)}, /*index=5*/s32[]{:T(128)}, s32[]{:T(128)}) %tuple.119), condition=%wide.region_12.13_spmd, body=%wide.region_11.12_spmd.sunk | while | flops 32774 | bytes 917671 | solution.py:136
  228.5 5.8 %collective-permute-done.2 = f32[128,256]{1,0:T(8,128)S(1)} collective-permute-done((f32[128,256]{1,0:T(8,128)S(1)}, f32[128,256]{1,0:T(8,128)S(1)}, u32[]{:S(2)}, u32[]{:S(2)}) %collective-permute-start.2) | collective-permute-done | bytes 131104 | tf_op jit(solution)/shard_map/while/body/eval_jaxpr/ppermute | solution.py:12
  236.5 6.9 %collective-permute-done.2 = f32[128,256]{1,0:T(8,128)S(1)} collective-permute-done((f32[128,256]{1,0:T(8,128)S(1)}, f32[128,256]{1,0:T(8,128)S(1)}, u32[]{:S(2)}, u32[]{:S(2)}) %collective-permute-start.2) | collective-permute-done | bytes 131104 | tf_op jit(solution)/shard_map/while/body/eval_jaxpr/ppermute | solution.py:12
  245.6 5.8 %collective-permute-done.2 = f32[128,256]{1,0:T(8,128)S(1)} collective-permute-done((f32[128,256]{1,0:T(8,128)S(1)}, f32[128,256]{1,0:T(8,128)S(1)}, u32[]{:S(2)}, u32[]{:S(2)}) %collective-permute-start.2) | collective-permute-done | bytes 131104 | tf_op jit(solution)/shard_map/while/body/eval_jaxpr/ppermute | solution.py:12
  253.6 7.7 %collective-permute-done.2 = f32[128,256]{1,0:T(8,128)S(1)} collective-permute-done((f32[128,256]{1,0:T(8,128)S(1)}, f32[128,256]{1,0:T(8,128)S(1)}, u32[]{:S(2)}, u32[]{:S(2)}) %collective-permute-start.2) | collective-permute-done | bytes 131104 | tf_op jit(solution)/shard_map/while/body/eval_jaxpr/ppermute | solution.py:12
  263.5 7.7 %collective-permute-done.2 = f32[128,256]{1,0:T(8,128)S(1)} collective-permute-done((f32[128,256]{1,0:T(8,128)S(1)}, f32[128,256]{1,0:T(8,128)S(1)}, u32[]{:S(2)}, u32[]{:S(2)}) %collective-permute-start.2) | collective-permute-done | bytes 131104 | tf_op jit(solution)/shard_map/while/body/eval_jaxpr/ppermute | solution.py:12
  273.4 8.9 %collective-permute-done.2 = f32[128,256]{1,0:T(8,128)S(1)} collective-permute-done((f32[128,256]{1,0:T(8,128)S(1)}, f32[128,256]{1,0:T(8,128)S(1)}, u32[]{:S(2)}, u32[]{:S(2)}) %collective-permute-start.2) | collective-permute-done | bytes 131104 | tf_op jit(solution)/shard_map/while/body/eval_jaxpr/ppermute | solution.py:12
  284.6 9.1 %collective-permute-done.2 = f32[128,256]{1,0:T(8,128)S(1)} collective-permute-done((f32[128,256]{1,0:T(8,128)S(1)}, f32[128,256]{1,0:T(8,128)S(1)}, u32[]{:S(2)}, u32[]{:S(2)}) %collective-permute-start.2) | collective-permute-done | bytes 131104 | tf_op jit(solution)/shard_map/while/body/eval_jaxpr/ppermute | solution.py:12
  295.9 7.4 %collective-permute-done.2 = f32[128,256]{1,0:T(8,128)S(1)} collective-permute-done((f32[128,256]{1,0:T(8,128)S(1)}, f32[128,256]{1,0:T(8,128)S(1)}, u32[]{:S(2)}, u32[]{:S(2)}) %collective-permute-start.2) | collective-permute-done | bytes 131104 | tf_op jit(solution)/shard_map/while/body/eval_jaxpr/ppermute | solution.py:12
  305.6 7.1 %collective-permute-done.2 = f32[128,256]{1,0:T(8,128)S(1)} collective-permute-done((f32[128,256]{1,0:T(8,128)S(1)}, f32[128,256]{1,0:T(8,128)S(1)}, u32[]{:S(2)}, u32[]{:S(2)}) %collective-permute-start.2) | collective-permute-done | bytes 131104 | tf_op jit(solution)/shard_map/while/body/eval_jaxpr/ppermute | solution.py:12
  314.9 7.4 %collective-permute-done.2 = f32[128,256]{1,0:T(8,128)S(1)} collective-permute-done((f32[128,256]{1,0:T(8,128)S(1)}, f32[128,256]{1,0:T(8,128)S(1)}, u32[]{:S(2)}, u32[]{:S(2)}) %collective-permute-start.2) | collective-permute-done | bytes 131104 | tf_op jit(solution)/shard_map/while/body/eval_jaxpr/ppermute | solution.py:12
  324.5 7.7 %collective-permute-done.2 = f32[128,256]{1,0:T(8,128)S(1)} collective-permute-done((f32[128,256]{1,0:T(8,128)S(1)}, f32[128,256]{1,0:T(8,128)S(1)}, u32[]{:S(2)}, u32[]{:S(2)}) %collective-permute-start.2) | collective-permute-done | bytes 131104 | tf_op jit(solution)/shard_map/while/body/eval_jaxpr/ppermute | solution.py:12
  334.4 7.7 %collective-permute-done.2 = f32[128,256]{1,0:T(8,128)S(1)} collective-permute-done((f32[128,256]{1,0:T(8,128)S(1)}, f32[128,256]{1,0:T(8,128)S(1)}, u32[]{:S(2)}, u32[]{:S(2)}) %collective-permute-start.2) | collective-permute-done | bytes 131104 | tf_op jit(solution)/shard_map/while/body/eval_jaxpr/ppermute | solution.py:12
  344.3 7.7 %collective-permute-done.2 = f32[128,256]{1,0:T(8,128)S(1)} collective-permute-done((f32[128,256]{1,0:T(8,128)S(1)}, f32[128,256]{1,0:T(8,128)S(1)}, u32[]{:S(2)}, u32[]{:S(2)}) %collective-permute-start.2) | collective-permute-done | bytes 131104 | tf_op jit(solution)/shard_map/while/body/eval_jaxpr/ppermute | solution.py:12
  354.2 7.7 %collective-permute-done.2 = f32[128,256]{1,0:T(8,128)S(1)} collective-permute-done((f32[128,256]{1,0:T(8,128)S(1)}, f32[128,256]{1,0:T(8,128)S(1)}, u32[]{:S(2)}, u32[]{:S(2)}) %collective-permute-start.2) | collective-permute-done | bytes 131104 | tf_op jit(solution)/shard_map/while/body/eval_jaxpr/ppermute | solution.py:12
  364.1 7.7 %collective-permute-done.2 = f32[128,256]{1,0:T(8,128)S(1)} collective-permute-done((f32[128,256]{1,0:T(8,128)S(1)}, f32[128,256]{1,0:T(8,128)S(1)}, u32[]{:S(2)}, u32[]{:S(2)}) %collective-permute-start.2) | collective-permute-done | bytes 131104 | tf_op jit(solution)/shard_map/while/body/eval_jaxpr/ppermute | solution.py:12
  374.0 7.7 %collective-permute-done.2 = f32[128,256]{1,0:T(8,128)S(1)} collective-permute-done((f32[128,256]{1,0:T(8,128)S(1)}, f32[128,256]{1,0:T(8,128)S(1)}, u32[]{:S(2)}, u32[]{:S(2)}) %collective-permute-start.2) | collective-permute-done | bytes 131104 | tf_op jit(solution)/shard_map/while/body/eval_jaxpr/ppermute | solution.py:12
  383.9 6.6 %convolution_convert_fusion = bf16[128,12288]{1,0:T(8,128)(2,1)} fusion(bf16[12288,256]{1,0:T(8,128)(2,1)} %all-gather.2.cloned.1.call-done, bf16[128,128]{0,1:T(8,128)(2,1)S(1)} %get-tuple-element.381, bf16[128,128]{0,1:T(8,128)(2,1)S(1)} %fusion.31), kind=kOutput, calls=%fused_computation.35 | convolution fusion | flops 807010304 | bytes 9502720 | tf_op jit(solution)/shard_map/dot_general | solution.py:150
  393.1 86.5 %reduce-scatter.2.cloned.1.call-done = bf16[16,12288]{1,0:T(8,128)(2,1)} async-done(((bf16[128,12288]{1,0:T(8,128)(2,1)}), bf16[16,12288]{1,0:T(8,128)(2,1)}) %reduce-scatter.2.cloned.1.call-update) | async-done | bytes 393232 | tf_op jit(solution)/shard_map/reduce_scatter | solution.py:149
  (305 shorter events, 247.2 us)
Async XLA Ops:
  7.2 376.8 %all-gather.2.cloned.1.call-start = ((), (), s32[]{:S(2)}) async-start(), calls=%async_computation.1 | async-start | bytes 6389760 | tf_op jit(solution)/shard_map/all_gather | solution.py:148
  7.9 471.7 %reduce-scatter.2.cloned.1.call-start = ((), (), s32[]{:S(2)}) async-start(), calls=%async_computation.2 | async-start | bytes 3538944 | tf_op jit(solution)/shard_map/reduce_scatter | solution.py:149
  30.9 11.0 %collective-permute-start = (bf16[128,256]{1,0:T(8,128)(2,1)S(1)}, bf16[128,256]{1,0:T(8,128)(2,1)S(1)}, u32[]{:S(2)}, u32[]{:S(2)}) collective-permute-start(bf16[128,256]{1,0:T(8,128)(2,1)S(1)} %get-tuple-element.551), channel_id=1, source_target_pairs={{0,8},{8,16},{16,24},{24,32},{32,40},{40,48},{48,56},{56,64},{64,7... | collective-permute-start | bytes 196616 | tf_op jit(solution)/shard_map/while/body/eval_jaxpr/ppermute | solution.py:12
  42.5 9.6 %collective-permute-start = (bf16[128,256]{1,0:T(8,128)(2,1)S(1)}, bf16[128,256]{1,0:T(8,128)(2,1)S(1)}, u32[]{:S(2)}, u32[]{:S(2)}) collective-permute-start(bf16[128,256]{1,0:T(8,128)(2,1)S(1)} %get-tuple-element.551), channel_id=1, source_target_pairs={{0,8},{8,16},{16,24},{24,32},{32,40},{40,48},{48,56},{56,64},{64,7... | collective-permute-start | bytes 196616 | tf_op jit(solution)/shard_map/while/body/eval_jaxpr/ppermute | solution.py:12
  52.7 9.5 %collective-permute-start = (bf16[128,256]{1,0:T(8,128)(2,1)S(1)}, bf16[128,256]{1,0:T(8,128)(2,1)S(1)}, u32[]{:S(2)}, u32[]{:S(2)}) collective-permute-start(bf16[128,256]{1,0:T(8,128)(2,1)S(1)} %get-tuple-element.551), channel_id=1, source_target_pairs={{0,8},{8,16},{16,24},{24,32},{32,40},{40,48},{48,56},{56,64},{64,7... | collective-permute-start | bytes 196616 | tf_op jit(solution)/shard_map/while/body/eval_jaxpr/ppermute | solution.py:12
  62.9 9.5 %collective-permute-start = (bf16[128,256]{1,0:T(8,128)(2,1)S(1)}, bf16[128,256]{1,0:T(8,128)(2,1)S(1)}, u32[]{:S(2)}, u32[]{:S(2)}) collective-permute-start(bf16[128,256]{1,0:T(8,128)(2,1)S(1)} %get-tuple-element.551), channel_id=1, source_target_pairs={{0,8},{8,16},{16,24},{24,32},{32,40},{40,48},{48,56},{56,64},{64,7... | collective-permute-start | bytes 196616 | tf_op jit(solution)/shard_map/while/body/eval_jaxpr/ppermute | solution.py:12
  73.0 9.5 %collective-permute-start = (bf16[128,256]{1,0:T(8,128)(2,1)S(1)}, bf16[128,256]{1,0:T(8,128)(2,1)S(1)}, u32[]{:S(2)}, u32[]{:S(2)}) collective-permute-start(bf16[128,256]{1,0:T(8,128)(2,1)S(1)} %get-tuple-element.551), channel_id=1, source_target_pairs={{0,8},{8,16},{16,24},{24,32},{32,40},{40,48},{48,56},{56,64},{64,7... | collective-permute-start | bytes 196616 | tf_op jit(solution)/shard_map/while/body/eval_jaxpr/ppermute | solution.py:12
  83.2 9.7 %collective-permute-start = (bf16[128,256]{1,0:T(8,128)(2,1)S(1)}, bf16[128,256]{1,0:T(8,128)(2,1)S(1)}, u32[]{:S(2)}, u32[]{:S(2)}) collective-permute-start(bf16[128,256]{1,0:T(8,128)(2,1)S(1)} %get-tuple-element.551), channel_id=1, source_target_pairs={{0,8},{8,16},{16,24},{24,32},{32,40},{40,48},{48,56},{56,64},{64,7... | collective-permute-start | bytes 196616 | tf_op jit(solution)/shard_map/while/body/eval_jaxpr/ppermute | solution.py:12
  93.5 10.4 %collective-permute-start = (bf16[128,256]{1,0:T(8,128)(2,1)S(1)}, bf16[128,256]{1,0:T(8,128)(2,1)S(1)}, u32[]{:S(2)}, u32[]{:S(2)}) collective-permute-start(bf16[128,256]{1,0:T(8,128)(2,1)S(1)} %get-tuple-element.551), channel_id=1, source_target_pairs={{0,8},{8,16},{16,24},{24,32},{32,40},{40,48},{48,56},{56,64},{64,7... | collective-permute-start | bytes 196616 | tf_op jit(solution)/shard_map/while/body/eval_jaxpr/ppermute | solution.py:12
  104.6 9.7 %collective-permute-start = (bf16[128,256]{1,0:T(8,128)(2,1)S(1)}, bf16[128,256]{1,0:T(8,128)(2,1)S(1)}, u32[]{:S(2)}, u32[]{:S(2)}) collective-permute-start(bf16[128,256]{1,0:T(8,128)(2,1)S(1)} %get-tuple-element.551), channel_id=1, source_target_pairs={{0,8},{8,16},{16,24},{24,32},{32,40},{40,48},{48,56},{56,64},{64,7... | collective-permute-start | bytes 196616 | tf_op jit(solution)/shard_map/while/body/eval_jaxpr/ppermute | solution.py:12
  114.9 9.6 %collective-permute-start = (bf16[128,256]{1,0:T(8,128)(2,1)S(1)}, bf16[128,256]{1,0:T(8,128)(2,1)S(1)}, u32[]{:S(2)}, u32[]{:S(2)}) collective-permute-start(bf16[128,256]{1,0:T(8,128)(2,1)S(1)} %get-tuple-element.551), channel_id=1, source_target_pairs={{0,8},{8,16},{16,24},{24,32},{32,40},{40,48},{48,56},{56,64},{64,7... | collective-permute-start | bytes 196616 | tf_op jit(solution)/shard_map/while/body/eval_jaxpr/ppermute | solution.py:12
  125.2 10.2 %collective-permute-start = (bf16[128,256]{1,0:T(8,128)(2,1)S(1)}, bf16[128,256]{1,0:T(8,128)(2,1)S(1)}, u32[]{:S(2)}, u32[]{:S(2)}) collective-permute-start(bf16[128,256]{1,0:T(8,128)(2,1)S(1)} %get-tuple-element.551), channel_id=1, source_target_pairs={{0,8},{8,16},{16,24},{24,32},{32,40},{40,48},{48,56},{56,64},{64,7... | collective-permute-start | bytes 196616 | tf_op jit(solution)/shard_map/while/body/eval_jaxpr/ppermute | solution.py:12
  136.0 10.7 %collective-permute-start = (bf16[128,256]{1,0:T(8,128)(2,1)S(1)}, bf16[128,256]{1,0:T(8,128)(2,1)S(1)}, u32[]{:S(2)}, u32[]{:S(2)}) collective-permute-start(bf16[128,256]{1,0:T(8,128)(2,1)S(1)} %get-tuple-element.551), channel_id=1, source_target_pairs={{0,8},{8,16},{16,24},{24,32},{32,40},{40,48},{48,56},{56,64},{64,7... | collective-permute-start | bytes 196616 | tf_op jit(solution)/shard_map/while/body/eval_jaxpr/ppermute | solution.py:12
  147.4 10.7 %collective-permute-start = (bf16[128,256]{1,0:T(8,128)(2,1)S(1)}, bf16[128,256]{1,0:T(8,128)(2,1)S(1)}, u32[]{:S(2)}, u32[]{:S(2)}) collective-permute-start(bf16[128,256]{1,0:T(8,128)(2,1)S(1)} %get-tuple-element.551), channel_id=1, source_target_pairs={{0,8},{8,16},{16,24},{24,32},{32,40},{40,48},{48,56},{56,64},{64,7... | collective-permute-start | bytes 196616 | tf_op jit(solution)/shard_map/while/body/eval_jaxpr/ppermute | solution.py:12
  158.7 10.7 %collective-permute-start = (bf16[128,256]{1,0:T(8,128)(2,1)S(1)}, bf16[128,256]{1,0:T(8,128)(2,1)S(1)}, u32[]{:S(2)}, u32[]{:S(2)}) collective-permute-start(bf16[128,256]{1,0:T(8,128)(2,1)S(1)} %get-tuple-element.551), channel_id=1, source_target_pairs={{0,8},{8,16},{16,24},{24,32},{32,40},{40,48},{48,56},{56,64},{64,7... | collective-permute-start | bytes 196616 | tf_op jit(solution)/shard_map/while/body/eval_jaxpr/ppermute | solution.py:12
  170.1 10.7 %collective-permute-start = (bf16[128,256]{1,0:T(8,128)(2,1)S(1)}, bf16[128,256]{1,0:T(8,128)(2,1)S(1)}, u32[]{:S(2)}, u32[]{:S(2)}) collective-permute-start(bf16[128,256]{1,0:T(8,128)(2,1)S(1)} %get-tuple-element.551), channel_id=1, source_target_pairs={{0,8},{8,16},{16,24},{24,32},{32,40},{40,48},{48,56},{56,64},{64,7... | collective-permute-start | bytes 196616 | tf_op jit(solution)/shard_map/while/body/eval_jaxpr/ppermute | solution.py:12
  252.3 9.0 %collective-permute-start.2 = (f32[128,256]{1,0:T(8,128)S(1)}, f32[128,256]{1,0:T(8,128)S(1)}, u32[]{:S(2)}, u32[]{:S(2)}) collective-permute-start(f32[128,256]{1,0:T(8,128)S(1)} %bitcast_add_fusion.2), channel_id=1, source_target_pairs={{8,0},{16,8},{24,16},{32,24},{40,32},{48,40},{56,48},{64,56},{72,6... | collective-permute-start | bytes 393224 | tf_op jit(solution)/shard_map/while/body/eval_jaxpr/ppermute | solution.py:12
  262.2 9.0 %collective-permute-start.2 = (f32[128,256]{1,0:T(8,128)S(1)}, f32[128,256]{1,0:T(8,128)S(1)}, u32[]{:S(2)}, u32[]{:S(2)}) collective-permute-start(f32[128,256]{1,0:T(8,128)S(1)} %bitcast_add_fusion.2), channel_id=1, source_target_pairs={{8,0},{16,8},{24,16},{32,24},{40,32},{48,40},{56,48},{64,56},{72,6... | collective-permute-start | bytes 393224 | tf_op jit(solution)/shard_map/while/body/eval_jaxpr/ppermute | solution.py:12
  272.1 10.2 %collective-permute-start.2 = (f32[128,256]{1,0:T(8,128)S(1)}, f32[128,256]{1,0:T(8,128)S(1)}, u32[]{:S(2)}, u32[]{:S(2)}) collective-permute-start(f32[128,256]{1,0:T(8,128)S(1)} %bitcast_add_fusion.2), channel_id=1, source_target_pairs={{8,0},{16,8},{24,16},{32,24},{40,32},{48,40},{56,48},{64,56},{72,6... | collective-permute-start | bytes 393224 | tf_op jit(solution)/shard_map/while/body/eval_jaxpr/ppermute | solution.py:12
  283.3 10.4 %collective-permute-start.2 = (f32[128,256]{1,0:T(8,128)S(1)}, f32[128,256]{1,0:T(8,128)S(1)}, u32[]{:S(2)}, u32[]{:S(2)}) collective-permute-start(f32[128,256]{1,0:T(8,128)S(1)} %bitcast_add_fusion.2), channel_id=1, source_target_pairs={{8,0},{16,8},{24,16},{32,24},{40,32},{48,40},{56,48},{64,56},{72,6... | collective-permute-start | bytes 393224 | tf_op jit(solution)/shard_map/while/body/eval_jaxpr/ppermute | solution.py:12
  333.1 9.0 %collective-permute-start.2 = (f32[128,256]{1,0:T(8,128)S(1)}, f32[128,256]{1,0:T(8,128)S(1)}, u32[]{:S(2)}, u32[]{:S(2)}) collective-permute-start(f32[128,256]{1,0:T(8,128)S(1)} %bitcast_add_fusion.2), channel_id=1, source_target_pairs={{8,0},{16,8},{24,16},{32,24},{40,32},{48,40},{56,48},{64,56},{72,6... | collective-permute-start | bytes 393224 | tf_op jit(solution)/shard_map/while/body/eval_jaxpr/ppermute | solution.py:12
  343.0 9.0 %collective-permute-start.2 = (f32[128,256]{1,0:T(8,128)S(1)}, f32[128,256]{1,0:T(8,128)S(1)}, u32[]{:S(2)}, u32[]{:S(2)}) collective-permute-start(f32[128,256]{1,0:T(8,128)S(1)} %bitcast_add_fusion.2), channel_id=1, source_target_pairs={{8,0},{16,8},{24,16},{32,24},{40,32},{48,40},{56,48},{64,56},{72,6... | collective-permute-start | bytes 393224 | tf_op jit(solution)/shard_map/while/body/eval_jaxpr/ppermute | solution.py:12
  352.9 9.0 %collective-permute-start.2 = (f32[128,256]{1,0:T(8,128)S(1)}, f32[128,256]{1,0:T(8,128)S(1)}, u32[]{:S(2)}, u32[]{:S(2)}) collective-permute-start(f32[128,256]{1,0:T(8,128)S(1)} %bitcast_add_fusion.2), channel_id=1, source_target_pairs={{8,0},{16,8},{24,16},{32,24},{40,32},{48,40},{56,48},{64,56},{72,6... | collective-permute-start | bytes 393224 | tf_op jit(solution)/shard_map/while/body/eval_jaxpr/ppermute | solution.py:12
  362.8 9.0 %collective-permute-start.2 = (f32[128,256]{1,0:T(8,128)S(1)}, f32[128,256]{1,0:T(8,128)S(1)}, u32[]{:S(2)}, u32[]{:S(2)}) collective-permute-start(f32[128,256]{1,0:T(8,128)S(1)} %bitcast_add_fusion.2), channel_id=1, source_target_pairs={{8,0},{16,8},{24,16},{32,24},{40,32},{48,40},{56,48},{64,56},{72,6... | collective-permute-start | bytes 393224 | tf_op jit(solution)/shard_map/while/body/eval_jaxpr/ppermute | solution.py:12
  (42 other events, 561.0 us)
Sparse Core Ops, SparseCore 0:
  11.3 91.8 all-gather.1
  390.7 88.8 reduce-scatter.1
where the time goes:
time: 491 us; the launch traced here: 486 us
  waiting for transfers between devices  228 us (46%)
  starting transfers between devices  158 us (32%)
  matrix products  34.7 us (7%)
  local copies, waits for them, and re-layouts  29.1 us (6%)
  other arithmetic  21.7 us (4%)
  between operations  14.3 us (3%)
    ppermute x48, starting transfers between devices, from_behind(): return lax.ppermute(value, axis, pairs)  158 us
    ppermute x48, waiting for transfers between devices, from_behind(): return lax.ppermute(value, axis, pairs)  140 us
    reduce_scatter x1, waiting for transfers between devices, local(): lax.psum_scatter(lax.dot_general(grad_rows, full_weight, (((1,), (1,)), (...  86.5 us
    add x16, other arithmetic, send_back(): return from_behind(acc + addend, 'ctx', -1)  14.8 us
    dot_general x5, matrix products, block_grads(): jnp.einsum('gqk,kd->qgd', dscore, keys, preferred_element_type=jnp.float32)  10.2 us
    dynamic_update_slice x16, local copies, waits for them, and re-layouts, carry_on(): stack = lax.dynamic_update_index_in_dim(stack, moving, step, 0)  10 us
  transfers between devices with their start and end apart: 50, of which 33 were waited for; matrix products, arithmetic and copies ran while one was open for 16% of the time, Pallas kernels for 0%

commit v1 on v0

v1 whole, which is shorter than its diff:
```python
import functools
import jax
import jax.numpy as jnp
import numpy as np
from jax import lax
from jax.experimental import pallas as pl
from jax.experimental.pallas import tpu as pltpu
from jax.sharding import PartitionSpec as P

HEAD = 128
TOK = 128
NX = 4
REACH = 4
LOG2E = 1.4426950408889634
NEG = -1e30
MESH = pl.DeviceIdType.MESH
NT = (((1,), (1,)), ((), ()))
NN = (((1,), (0,)), ((), ()))
f32 = jnp.float32
bf16 = jnp.bfloat16


def dot(a, b, dims):
    return lax.dot_general(a, b, dims, preferred_element_type=f32)


def kernel(
    nc, nz, nx, ny, group, rb,
    q_ref, k_ref, v_ref, o_ref, do_ref, lab_ref, w_ref, inv_ref,
    dq_ref, dk_ref, dv_ref, dx_ref,
    qs, dos, kbuf, vbuf, kt, labown, labs, sbuf, bias, mrow, lrow, frow, dqt, acc,
    outbox, own32, rx, zout, rz, gloc, gy, gall, obuf, oin, wf, ssem, rsem,
):
    c = lax.axis_index("dp")
    ctx = lax.axis_index("ctx")
    y = lax.axis_index("tp")
    z, x = lax.div(ctx, nx), lax.rem(ctx, nx)
    scale = HEAD ** (-0.5)
    planes = REACH + 1
    keys = nx * TOK
    piece = TOK // ny
    count = [0]
    sends = []

    def at_z(d):
        return {"ctx": lax.rem(z + d + nz, nz) * nx + x}

    def at_x(d):
        return {"ctx": z * nx + lax.rem(x + d, nx)}

    def at_y(d):
        return {"tp": lax.rem(y + d + ny, ny)}

    def send(src, dst, device):
        n = count[0]
        count[0] = n + 1
        copy = pltpu.make_async_remote_copy(
            src_ref=src, dst_ref=dst, send_sem=ssem.at[n], recv_sem=rsem.at[n],
            device_id=device, device_id_type=MESH,
        )
        copy.start()
        sends.append(copy)
        return copy

    def rows(i, n):
        return pl.ds(pl.multiple_of(i * n, n), n)

    sibling = {"dp": 1 - c}
    peers = [at_z(d) for d in range(1, nz)] + [at_x(d) for d in range(1, nx)]
    peers += [at_y(d) for d in range(1, ny)] + ([sibling] if nc == 2 else [])
    barrier = pltpu.get_barrier_semaphore()
    for peer in peers:
        pl.semaphore_signal(barrier, inc=1, device_id=peer, device_id_type=MESH)
    pl.semaphore_wait(barrier, len(peers))

    mine = rows(x, TOK)
    own_lab = lab_ref[...]
    labown[...] = jnp.broadcast_to(own_lab, (8, TOK))
    labs[x, 0] = jnp.broadcast_to(own_lab, (8, TOK))
    lab_z = [send(labown, labs.at[x, s], at_z(s)) for s in range(1, planes)]
    kz = [None] + [send(k_ref.at[0], kbuf.at[s, mine], at_z(s)) for s in range(1, planes)]
    kx = {0: [send(k_ref.at[0], kbuf.at[0, mine], at_x(d)) for d in range(1, nx)]}
    vz = [None] + [send(v_ref.at[0], vbuf.at[s, mine], at_z(s)) for s in range(1, planes)]
    vx = {0: [send(v_ref.at[0], vbuf.at[0, mine], at_x(d)) for d in range(1, nx)]}
    wx = [send(w_ref, wf.at[y, c, x], at_x(d)) for d in range(1, nx)]
    kbuf[0, mine] = k_ref[0]
    vbuf[0, mine] = v_ref[0]
    wf[y, c, x] = w_ref[...]

    lane = lax.broadcasted_iota(jnp.int32, (TOK, HEAD), 1)
    for h in range(group):
        cols = slice(h * HEAD, (h + 1) * HEAD)
        part = slice(h * TOK, (h + 1) * TOK)
        qs[part, :] = q_ref[0, :, cols]
        grad = do_ref[0, :, cols]
        dos[part, 0:HEAD] = grad
        delta = -jnp.sum(
            grad.astype(f32) * o_ref[0, :, cols].astype(f32), axis=1, keepdims=True
        )
        high = delta.astype(bf16).astype(f32)
        middle = (delta - high).astype(bf16).astype(f32)
        low = delta - high - middle
        extra = jnp.where(lane == 0, high, jnp.where(lane == 1, middle, low))
        dos[part, HEAD:] = jnp.where(lane < 3, extra, 0.0).astype(bf16)

    dqt[...] = jnp.zeros_like(dqt)

    for copy in lab_z:
        copy.wait_recv()
    lab_x = [send(labs.at[x], labs.at[x], at_x(d)) for d in range(1, nx)]
    for copy in lab_x:
        copy.wait_recv()
    start = jnp.zeros((1, TOK), f32)
    for value in range(1, 4):
        tally = jnp.zeros((8, TOK), f32)
        for s in range(planes):
            here = jnp.zeros((8, TOK), f32)
            for other in range(nx):
                here += jnp.where(labs[other, s] < value, 1.0, 0.0)
            tally += here * jnp.where(z >= s, 1.0, 0.0)
        total = jnp.sum(tally, axis=1, keepdims=True)[0:1]
        start = jnp.where(own_lab == value, total, start)
    start = start + (jnp.maximum(z - REACH, 0) * keys).astype(f32)
    lane1 = lax.broadcasted_iota(jnp.int32, (1, TOK), 1)
    query_at = (lane1 + ctx * TOK).astype(f32)

    width = 2 * TOK
    chunks = group * TOK // width

    def pass_one(s):
        plane = lax.rem(z - s + nz, nz)
        key_at = (lax.broadcasted_iota(jnp.int32, (keys, TOK), 0) + plane * keys).astype(f32)
        allowed = (key_at >= start) & (key_at <= query_at)
        bias[...] = jnp.where(allowed, 0.0, NEG)

        def body(i, carry):
            part = rows(i, width)
            scores = dot(kbuf[s], qs[part, :], NT) * (scale * LOG2E)
            more = bias[...]
            scores = scores + jnp.concatenate([more, more], axis=1)
            top = jnp.max(scores, axis=0, keepdims=True)
            e = jnp.exp2(scores - top)
            sbuf[s, i] = e
            mrow[s : s + 1, part] = top
            lrow[s : s + 1, part] = jnp.sum(e, axis=0, keepdims=True)
            return carry

        lax.fori_loop(0, chunks, body, 0)

    wsteps = []

    def w_begin():
        for copy in wx:
            copy.wait_recv()
        up = send(wf.at[y, c], wf.at[y, c], at_y(1))
        down = send(wf.at[y, c], wf.at[y, c], at_y(-1))
        over = send(wf.at[y, c], wf.at[y, c], sibling) if nc == 2 else None
        wsteps.append((up, down, over))

    half = ny // 2

    def w_step(k):
        up, down, _ = wsteps[-1]
        from_up = lax.rem(y - k + ny, ny)
        from_down = lax.rem(y + k, ny)
        last = nx // 2
        up.wait_recv()
        new_up = new_down = None
        if k + 1 < half:
            new_up = send(wf.at[from_up, c], wf.at[from_up, c], at_y(1))
        elif k + 1 == half:
            new_up = send(
                wf.at[from_up, c, 0:last], wf.at[from_up, c, 0:last], at_y(1)
            )
        overs = []
        if down is not None:
            down.wait_recv()
        if k + 1 < half:
            new_down = send(wf.at[from_down, c], wf.at[from_down, c], at_y(-1))
        elif k + 1 == half:
            new_down = send(
                wf.at[from_down, c, last:nx], wf.at[from_down, c, last:nx], at_y(-1)
            )
        if nc == 2:
            overs.append(send(wf.at[from_up, c], wf.at[from_up, c], sibling))
            if k < half:
                overs.append(send(wf.at[from_down, c], wf.at[from_down, c], sibling))
        wsteps.append((new_up, new_down, overs))

    for s in range(planes):
        if s < REACH:
            kz[s + 1].wait_recv()
            kx[s + 1] = [
                send(kbuf.at[s + 1, mine], kbuf.at[s + 1, mine], at_x(d)) for d in range(1, nx)
            ]
        if s > 0:
            vz[s].wait_recv()
            vx[s] = [send(vbuf.at[s, mine], vbuf.at[s, mine], at_x(d)) for d in range(1, nx)]
        for copy in kx[s]:
            copy.wait_recv()
        pass_one(s)
        if s == 0:
            w_begin()

    top = jnp.max(mrow[0:planes, :], axis=0, keepdims=True)
    shift = mrow[0:planes, :] - top
    total = jnp.sum(lrow[0:planes, :] * jnp.exp2(shift), axis=0, keepdims=True)
    frow[0:planes, :] = jnp.exp2(shift - jnp.log2(total))

    ones = jnp.where(
        lax.broadcasted_iota(jnp.int32, (keys, HEAD), 1) < 3, 1.0, 0.0
    ).astype(bf16)

    def pass_two(s):
        kt[...] = kbuf[s].astype(f32).T.astype(bf16)
        acc[...] = jnp.zeros_like(acc)

        def body(i, carry):
            part = rows(i, width)
            prob = sbuf[s, i] * frow[s : s + 1, part]
            grads = dos[part, :]
            dprob = dot(jnp.concatenate([vbuf[s], ones], axis=1), grads, NT)
            dscore = (prob * dprob).astype(bf16)
            acc[:, HEAD:] += dot(prob.astype(bf16), grads[:, 0:HEAD], NN)
            acc[:, 0:HEAD] += dot(dscore, qs[part, :], NN)
            dqt[:, part] += dot(kt[...], dscore, NN)
            return carry

        lax.fori_loop(0, chunks, body, 0)
        acc[:, 0:HEAD] = acc[:, 0:HEAD] * scale
        for other in range(nx):
            outbox[s, other] = acc[other * TOK : (other + 1) * TOK, :].astype(bf16)
        own32[s] = acc[mine, :]

    def summed(s):
        total = own32[s]
        for copy in back_x[s]:
            copy.wait_recv()
        for d in range(nx - 1):
            total = total + rx[s, d].astype(f32)
        return total

    back_x, back_z = {}, []
    for s in range(REACH, -1, -1):
        for copy in vx[s]:
            copy.wait_recv()
        pass_two(s)
        back_x[s] = [
            send(outbox.at[s, lax.rem(x + d, nx)], rx.at[s, d - 1], at_x(d))
            for d in range(1, nx)
        ]
        if s < REACH:
            zout[s] = summed(s + 1).astype(bf16)
            back_z.append(send(zout.at[s], rz.at[s], at_z(-(s + 1))))
        if s == REACH - 1:
            w_step(1)
        if s == 1:
            w_step(2)

    for h in range(group):
        cols = slice(h * HEAD, (h + 1) * HEAD)
        dq_ref[0, :, cols] = (dqt[:, cols].T * scale).astype(bf16)

    row_at = (lax.broadcasted_iota(jnp.int32, (TOK, HEAD), 0) + ctx * TOK).astype(f32)
    angle = row_at * inv_ref[...]
    cosine, sine = jnp.cos(angle), jnp.sin(angle)

    total = summed(0)
    for copy in back_z:
        copy.wait_recv()
    for s in range(REACH):
        total = total + rz[s].astype(f32)
    key_sum = total[:, 0:HEAD]
    value_half = total[:, HEAD:].astype(bf16)
    dk_ref[0] = key_sum.astype(bf16)
    dv_ref[0] = value_half
    turned = pltpu.roll(key_sum, HEAD // 2, axis=1)
    turned = jnp.where(lane < HEAD // 2, -turned, turned)
    gloc[:, 0:HEAD] = (key_sum * cosine - turned * sine).astype(bf16)
    gloc[:, HEAD:] = value_half

    gy_in = [
        send(gloc.at[rows(lax.rem(y + d, ny), piece)], gy.at[y], at_y(d)) for d in range(1, ny)
    ]
    gy[y] = gloc[rows(y, piece), :]
    for copy in gy_in:
        copy.wait_recv()
    g_in = [send(gy, gall.at[z], at_z(d)) for d in range(1, nz)]
    gall[z] = gy[...]
    for k in range(3, half + 1):
        w_step(k)
    if nc == 2:
        wsteps[0][2].wait_recv()
        for _, _, overs in wsteps[1:]:
            for copy in overs:
                copy.wait_recv()
    for copy in g_in:
        copy.wait_recv()

    cols_each = nx * rb
    for core in range(nc):
        part = jnp.zeros((nz * piece, cols_each), f32)
        for h in range(ny):
            tokens = gall[:, h].reshape(nz * piece, 2 * HEAD)
            part = part + dot(tokens, wf[h, core].reshape(cols_each, 2 * HEAD), NT)
        obuf[:, :, core * cols_each : (core + 1) * cols_each] = part.astype(bf16).reshape(
            nz, piece, cols_each
        )
    o_in = [send(obuf.at[lax.rem(z + d, nz)], oin.at[z], at_z(d)) for d in range(1, nz)]
    oin[z] = obuf[z]
    for copy in o_in:
        copy.wait_recv()
    for core in range(nc):
        for m in range(nz):
            at = (core * nz + m) * cols_each
            dx_ref[0, :, at : at + cols_each] = oin[
                m, :, core * cols_each : (core + 1) * cols_each
            ]
    for copy in sends:
        copy.wait_send()


def local(sizes, q, k, v, o, do, lab, w):
    nc, nz, nx, ny = sizes
    group = q.shape[-1] // HEAD
    rb = w.shape[0]
    planes, keys, piece = REACH + 1, nx * TOK, TOK // ny
    d_all = rb * nc * nz * nx
    half = HEAD // 2
    inv = np.exp(
        -np.log(np.float32(1000000.0)) * (np.float32(2.0) * np.arange(half, dtype=np.float32) / HEAD)
    ).astype(np.float32)
    inv = jnp.asarray(np.concatenate([inv, inv])[None, :])
    copies = 160
    vm = pltpu.VMEM
    scratch = [
        vm((group * TOK, HEAD), bf16),
        vm((group * TOK, 2 * HEAD), bf16),
        vm((planes, keys, HEAD), bf16),
        vm((planes, keys, HEAD), bf16),
        vm((HEAD, keys), bf16),
        vm((8, TOK), jnp.int32),
        vm((nx, planes, 8, TOK), jnp.int32),
        vm((planes, group // 2, keys, 2 * TOK), f32),
        vm((keys, TOK), f32),
        vm((8, group * TOK), f32),
        vm((8, group * TOK), f32),
        vm((8, group * TOK), f32),
        vm((HEAD, group * TOK), f32),
        vm((keys, 2 * HEAD), f32),
        vm((planes, nx, TOK, 2 * HEAD), bf16),
        vm((planes, TOK, 2 * HEAD), f32),
        vm((planes, nx - 1, TOK, 2 * HEAD), bf16),
        vm((REACH, TOK, 2 * HEAD), bf16),
        vm((REACH, TOK, 2 * HEAD), bf16),
        vm((TOK, 2 * HEAD), bf16),
        vm((ny, piece, 2 * HEAD), bf16),
        vm((nz, ny, piece, 2 * HEAD), bf16),
        vm((nz, piece, nc * nx * rb), bf16),
        vm((nz, piece, nc * nx * rb), bf16),
        vm((ny, nc, nx, rb, 2 * HEAD), bf16),
        pltpu.SemaphoreType.DMA((copies,)),
        pltpu.SemaphoreType.DMA((copies,)),
    ]
    spec = pl.BlockSpec(memory_space=pltpu.VMEM)
    return pl.pallas_call(
        functools.partial(kernel, nc, nz, nx, ny, group, rb),
        out_shape=(
            jax.ShapeDtypeStruct(q.shape, bf16),
            jax.ShapeDtypeStruct(k.shape, bf16),
            jax.ShapeDtypeStruct(v.shape, bf16),
            jax.ShapeDtypeStruct((1, piece, d_all), bf16),
        ),
        in_specs=[spec] * 8,
        out_specs=(spec,) * 4,
        scratch_shapes=scratch,
        compiler_params=pltpu.CompilerParams(
            collective_id=0, has_side_effects=True, vmem_limit_bytes=56 * 1024 * 1024
        ),
    )(q, k, v, o, do, lab, w, inv)


def solution(mesh):
    nx = NX
    sizes = (mesh.shape["dp"], mesh.shape["ctx"] // nx, nx, mesh.shape["tp"])
    in_specs = (
        P("dp", "ctx", "tp"),
        P("dp", "ctx", "tp"),
        P("dp", "ctx", "tp"),
        P("dp", "ctx", "tp"),
        P("dp", "ctx", "tp"),
        P("dp", "ctx"),
        P(("dp", "ctx"), "tp"),
    )
    out_specs = (
        P("dp", "ctx", "tp"),
        P("dp", "ctx", "tp"),
        P("dp", "ctx", "tp"),
        P("dp", ("ctx", "tp"), None),
    )
    return jax.shard_map(
        functools.partial(local, sizes),
        mesh=mesh, in_specs=in_specs, out_specs=out_specs, check_vma=False,
    )
```

time: 491 us -> 103 us (0.21)
  waiting for transfers between devices: 228 us -> 0 us
  starting transfers between devices: 158 us -> 0 us
  Pallas kernels: 0 us -> 97.8 us
  matrix products: 34.7 us -> 0 us
  local copies, waits for them, and re-layouts: 29.1 us -> 3.96 us
  other arithmetic: 21.7 us -> 0 us
  between operations: 14.3 us -> 0.66 us
    ppermute x48 -> x0, starting transfers between devices: 158 us -> none  [from_behind(): return lax.ppermute(value, axis, pairs)]
    ppermute x48 -> x0, waiting for transfers between devices: 140 us -> none  [from_behind(): return lax.ppermute(value, axis, pairs)]
    pallas_call x0 -> x1, Pallas kernels: none -> 97.8 us  [local(): pl.pallas_call(functools.partial(kernel, nc, nz, nx, ny, group, rb), out_...]
    reduce_scatter x1 -> x0, waiting for transfers between devices: 86.5 us -> none  [local(): lax.psum_scatter(lax.dot_general(grad_rows, full_weight, (((1,), (1,)), (...]
    dot_general x30 -> x0, matrix products: 34.7 us -> none  [the longest x5 10.2 us: block_grads(): jnp.einsum('gqk,kd->qgd', dscore, keys, preferred_element_type=jnp.float32)]
    add x22 -> x0, other arithmetic: 14.8 us -> none  [the longest x16 14.8 us: send_back(): return from_behind(acc + addend, 'ctx', -1)]
    dynamic_update_slice x40 -> x0, local copies, waits for them, and re-layouts: 14.6 us -> none  [the longest x16 10 us: carry_on(): stack = lax.dynamic_update_index_in_dim(stack, moving, step, 0)]
    squeeze x8 -> x0, local copies, waits for them, and re-layouts: 8.37 us -> none  [local(): lax.scan(gather_stats, (top, total), (far_keys, far_labels))]
  transfers between devices with their start and end apart: 50 -> 0, of which waited for: 33 -> 0; matrix products, arithmetic and copies ran while one was open for 16% -> 0% of each run, Pallas kernels for 0% -> 0%
where the time goes in v1:
time: 103 us; the launch traced here: 102 us
  Pallas kernels  97.8 us (95%)
  local copies, waits for them, and re-layouts  3.96 us (4%)
    pallas_call x1, Pallas kernels, local(): pl.pallas_call(functools.partial(kernel, nc, nz, nx, ny, group, rb), out_...  97.8 us
    unnamed x10, local copies, waits for them, and re-layouts  3.96 us

profile of v1, /device:TPU:56, one launch (start us, length us, event | category | flops | bytes accessed | tf_op | source)
XLA Modules:
  0.0 102.4 jit_solution(17451304477394304343)
XLA Ops:
  0.6 97.8 %shard_map.111 = (bf16[1,128,1536]{2,1,0:T(8,128)(2,1)}, bf16[1,128,128]{2,1,0:T(8,128)(2,1)}, bf16[1,128,128]{2,1,0:T(8,128)(2,1)}, bf16[1,16,12288]{2,1,0:T(8,128)(2,1)}) custom-call(bf16[1,128,1536]{2,1,0:T(8,128)(2,1)} %q_ref.1, bf16[1,128,128]{2,1,0:T(8,128)(2,1)} %k_ref.1, bf16[1,128,128]{2,1,0:T(8,128)(2,1)} %v_ref.1, bf16[1,128,1536]{2,1,0:T(8,128)(2,1)} %o_ref.1, ...), custom_call_target="tpu_custom_call" | custom-call | tf_op jit(solution)/shard_map/pallas_call | solution.py:366
  98.4 0.0 copy-start.2
  98.4 0.0 copy-start
  98.4 1.8 %copy.16 = bf16[1,128,1536]{2,1,0:T(8,128)(2,1)} copy(bf16[1,128,1536]{2,1,0:T(8,128)(2,1)} %get-tuple-element.8) | data formatting | bytes 786432
  100.2 0.0 copy-done.2
  100.2 0.0 copy-start.1
  100.2 0.6 copy.17
  100.9 0.2 copy-done.1
  101.0 0.6 copy.18
  101.6 0.0 copy-done
  101.6 0.7 copy.19
Async XLA Ops:
  98.4 1.8 %copy-start.2 = (bf16[1,128,128]{2,1,0:T(8,128)(2,1)S(1)}, bf16[1,128,128]{2,1,0:T(8,128)(2,1)}, u32[]{:S(2)}) copy-start(bf16[1,128,128]{2,1,0:T(8,128)(2,1)} %get-tuple-element.9) | copy-start | bytes 98308
  98.4 3.2 %copy-start = (bf16[1,16,12288]{2,1,0:T(8,128)(2,1)S(1)}, bf16[1,16,12288]{2,1,0:T(8,128)(2,1)}, u32[]{:S(2)}) copy-start(bf16[1,16,12288]{2,1,0:T(8,128)(2,1)} %get-tuple-element.11) | copy-start | bytes 1179652
  100.2 0.8 copy-start.1

commit v2 on v1

v2 whole, which is shorter than its diff:
```python
import functools
import jax
import jax.numpy as jnp
import numpy as np
from jax import lax
from jax.experimental import pallas as pl
from jax.experimental.pallas import tpu as pltpu
from jax.sharding import PartitionSpec as P

HEAD = 128
TOK = 128
NX = 4
REACH = 4
PACK = TOK + 16
LOG2E = 1.4426950408889634
NEG = -1e30
MESH = pl.DeviceIdType.MESH
NT = (((1,), (1,)), ((), ()))
NN = (((1,), (0,)), ((), ()))
f32 = jnp.float32
bf16 = jnp.bfloat16


def dot(a, b, dims):
    return lax.dot_general(a, b, dims, preferred_element_type=f32)


class Semaphores:
    def __init__(self):
        self.used = 0

    def take(self, count):
        first = self.used
        self.used += count
        return first


def kernel(
    nc, nz, nx, ny, group, rb,
    lab_ref, inv_ref, q_ref, k_ref, v_ref, o_ref, do_ref, w_ref,
    dq_ref, dk_ref, dv_ref, dx_ref,
    qin, oin0, doin, qs, dos, kbuf, vbuf, kt, sbuf, bias, mrow, lrow, frow, dqt, acc,
    outbox, own32, rx, zout, rz, gloc, gy, gall, obuf, oin, wf,
    dq_out, dk_out, dv_out, dx_out, ssem, rsem, lsem,
):
    c = lax.axis_index("dp")
    ctx = lax.axis_index("ctx")
    y = lax.axis_index("tp")
    z, x = lax.div(ctx, nx), lax.rem(ctx, nx)
    scale = HEAD ** (-0.5)
    planes = REACH + 1
    keys = nx * TOK
    piece = TOK // ny
    wide = group * TOK
    half = ny // 2
    slots = nz // 2
    sems = Semaphores()
    ends = []

    def at(dz, dx):
        return {"ctx": lax.rem(z + dz + nz, nz) * nx + lax.rem(x + dx, nx)}

    def at_y(d):
        return {"tp": lax.rem(y + d + ny, ny)}

    sibling = {"dp": 1 - c}
    odd = lax.rem(z, 2)
    other_z = 1 - 2 * odd
    members = [(dp, dx) for dp in range(2) for dx in range(nx) if dp + dx > 0]
    me = odd * nx + x

    def at_member(dp, dx):
        return at(dp * other_z, dx)

    def member(dp, dx):
        return lax.rem(odd + dp, 2) * nx + lax.rem(x + dx, nx)

    def remote(n, src, dst, device):
        return pltpu.make_async_remote_copy(
            src_ref=src, dst_ref=dst, send_sem=ssem.at[n], recv_sem=rsem.at[n],
            device_id=device, device_id_type=MESH,
        )

    def send(n, src, dst, device):
        remote(n, src, dst, device).start()

    def arrived(n, dst):
        remote(n, dst, dst, at_y(1)).wait_recv()

    def sent(n, src):
        remote(n, src, src, at_y(1)).wait_send()

    peers = [at(d, 0) for d in range(1, nz)] + [at(0, d) for d in range(1, nx)]
    peers += [at_member(1, dx) for dx in range(1, nx)]
    peers += [at_y(d) for d in range(1, ny)] + ([sibling] if nc == 2 else [])
    barrier = pltpu.get_barrier_semaphore()
    for peer in peers:
        pl.semaphore_signal(barrier, inc=1, device_id=peer, device_id_type=MESH)

    mine = pl.ds(pl.multiple_of(x * TOK, TOK), TOK)
    zslot = lax.div(z, 2)
    local_in = [
        pltpu.make_async_copy(src, dst, lsem.at[n])
        for n, (src, dst) in enumerate([
            (k_ref.at[0], kbuf.at[0, x, 0:TOK]),
            (v_ref.at[0], vbuf.at[0, mine]),
            (do_ref.at[0], doin),
            (o_ref.at[0], oin0),
            (q_ref.at[0], qin),
            (w_ref, wf.at[y, c, zslot]),
        ])
    ]
    for copy in local_in:
        copy.start()
    own_lab = lab_ref[...].astype(f32)
    kbuf[0, x, TOK:PACK] = jnp.broadcast_to(own_lab, (PACK - TOK, TOK)).astype(bf16)
    local_in[0].wait()
    local_in[1].wait()
    pl.semaphore_wait(barrier, len(peers))

    n_kz, n_vz = sems.take(planes), sems.take(planes)
    n_kx, n_vx = sems.take(planes * (nx - 1)), sems.take(planes * (nx - 1))

    def keys_x(s):
        for d in range(1, nx):
            send(n_kx + s * (nx - 1) + d - 1, kbuf.at[s, x], kbuf.at[s, x], at(0, d))

    def values_x(s):
        for d in range(1, nx):
            send(n_vx + s * (nx - 1) + d - 1, vbuf.at[s, mine], vbuf.at[s, mine], at(0, d))

    keys_x(0)
    for s in range(1, planes):
        send(n_kz + s, kbuf.at[0, x], kbuf.at[s, x], at(s, 0))
    wz = [(sems.take(1), d) for d in range(2, nz, 2)]
    for n, d in wz:
        send(n, w_ref, wf.at[y, c, zslot], at(d, 0))
    values_x(0)
    for s in range(1, planes):
        send(n_vz + s, vbuf.at[0, mine], vbuf.at[s, mine], at(s, 0))

    for copy in local_in[2:]:
        copy.wait()
    lane = lax.broadcasted_iota(jnp.int32, (TOK, HEAD), 1)
    for h in range(group):
        cols = slice(h * HEAD, (h + 1) * HEAD)
        part = slice(h * TOK, (h + 1) * TOK)
        qs[part, :] = qin[:, cols]
        grad = doin[:, cols]
        dos[part, 0:HEAD] = grad
        delta = -jnp.sum(
            grad.astype(f32) * oin0[:, cols].astype(f32), axis=1, keepdims=True
        )
        high = delta.astype(bf16).astype(f32)
        middle = (delta - high).astype(bf16).astype(f32)
        low = delta - high - middle
        extra = jnp.where(lane == 0, high, jnp.where(lane == 1, middle, low))
        dos[part, HEAD:] = jnp.where(lane < 3, extra, 0.0).astype(bf16)

    dqt[...] = jnp.zeros_like(dqt)
    row = lax.broadcasted_iota(jnp.int32, (TOK, TOK), 0)
    query_at = lane + ctx * TOK

    n_up, n_down, n_over = sems.take(half + 1), sems.take(half + 1), sems.take(2 * half + 2)
    split = slots // 2

    def ring_refs(d):
        low, high = lax.rem(y - d + ny, ny), lax.rem(y + d, ny)
        if d < half:
            return wf.at[low, c], wf.at[high, c]
        return wf.at[low, c, 0:split], wf.at[high, c, split:slots]

    def w_begin():
        for n, _ in wz:
            arrived(n, wf.at[y, c, 0])
        send(n_up + 1, wf.at[y, c], wf.at[y, c], at_y(1))
        send(n_down + 1, wf.at[y, c], wf.at[y, c], at_y(-1))
        if nc == 2:
            send(n_over, wf.at[y, c], wf.at[y, c], sibling)

    def w_step(d):
        low, high = ring_refs(d)
        arrived(n_up + d, low)
        if d < half:
            part = low if d + 1 < half else wf.at[lax.rem(y - d + ny, ny), c, 0:split]
            send(n_up + d + 1, part, part, at_y(1))
        arrived(n_down + d, high)
        if d < half:
            part = high if d + 1 < half else wf.at[lax.rem(y + d, ny), c, split:slots]
            send(n_down + d + 1, part, part, at_y(-1))
        if nc == 2:
            send(n_over + 2 * d, low, low, sibling)
            send(n_over + 2 * d + 1, high, high, sibling)

    def pass_one(s, carry):
        @pl.when(s < REACH)
        def _():
            arrived(n_kz + s + 1, kbuf.at[0, x])
            keys_x(s + 1)

        @pl.when(s > 0)
        def _():
            arrived(n_vz + s, vbuf.at[0, mine])
            values_x(s)

        for d in range(nx - 1):
            arrived(n_kx + s * (nx - 1) + d, kbuf.at[0, x])
        plane = lax.rem(z - s + nz, nz)
        for other in range(nx):
            labels = kbuf[s, other, TOK:PACK].astype(f32)[0:1]
            labels = jnp.broadcast_to(labels, (TOK, TOK)).T
            key_at = row + (plane * nx + other) * TOK
            allowed = (labels == own_lab) & (key_at <= query_at)
            bias[other * TOK : (other + 1) * TOK, :] = jnp.where(allowed, 0.0, NEG)
        block = jnp.concatenate([kbuf[s, other, 0:TOK] for other in range(nx)], axis=0)
        width = 2 * TOK
        for i in range(wide // width):
            part = slice(i * width, (i + 1) * width)
            scores = dot(block, qs[part, :], NT) * (scale * LOG2E)
            more = bias[...]
            scores = scores + jnp.concatenate([more, more], axis=1)
            top = jnp.max(scores, axis=0, keepdims=True)
            e = jnp.exp2(scores - top)
            sbuf[s, :, part] = e
            mrow[s, :, part] = top
            lrow[s, :, part] = jnp.sum(e, axis=0, keepdims=True)

        @pl.when(s == 1)
        def _():
            w_begin()

        return carry

    lax.fori_loop(0, planes, pass_one, 0)

    top = mrow[0]
    for s in range(1, planes):
        top = jnp.maximum(top, mrow[s])
    total = jnp.zeros_like(top)
    for s in range(planes):
        total = total + lrow[s] * jnp.exp2(mrow[s] - top)
    lse = top + jnp.log2(total)
    for s in range(planes):
        frow[s] = jnp.exp2(mrow[s] - lse)

    ones = jnp.where(
        lax.broadcasted_iota(jnp.int32, (keys, HEAD), 1) < 3, 1.0, 0.0
    ).astype(bf16)
    n_bx, n_bz = sems.take(planes * (nx - 1)), sems.take(planes)

    def summed(s):
        for d in range(nx - 1):
            arrived(n_bx + s * (nx - 1) + d, rx.at[0, 0])
        total = own32[s]
        for d in range(nx - 1):
            total = total + rx[s, d].astype(f32)
        return total

    def pass_two(r, carry):
        s = REACH - r
        for d in range(nx - 1):
            arrived(n_vx + s * (nx - 1) + d, vbuf.at[0, mine])
        block = jnp.concatenate([kbuf[s, other, 0:TOK] for other in range(nx)], axis=0)
        kt[...] = block.astype(f32).T.astype(bf16)
        prob = sbuf[s] * frow[s]
        dprob = dot(jnp.concatenate([vbuf[s], ones], axis=1), dos[...], NT)
        dscore = (prob * dprob).astype(bf16)
        acc[:, HEAD:] = dot(prob.astype(bf16), dos[:, 0:HEAD], NN)
        acc[:, 0:HEAD] = dot(dscore, qs[...], NN) * scale
        dqt[...] += dot(kt[...], dscore, NN)
        for other in range(nx):
            outbox[s, other] = acc[other * TOK : (other + 1) * TOK, :].astype(bf16)
        own32[s] = acc[mine, :]
        for d in range(1, nx):
            send(
                n_bx + s * (nx - 1) + d - 1,
                outbox.at[s, lax.rem(x + d, nx)], rx.at[s, d - 1], at(0, d),
            )

        @pl.when(s < REACH)
        def _():
            zout[s] = summed(s + 1).astype(bf16)
            send(n_bz + s, zout.at[s], rz.at[s], at(-(s + 1), 0))

        for d in range(1, half - 1):
            @pl.when(s == half - 2 - d)
            def _(d=d):
                w_step(d)

        return carry

    lax.fori_loop(0, planes, pass_two, 0)

    for h in range(group):
        cols = slice(h * HEAD, (h + 1) * HEAD)
        dq_out[0, :, cols] = (dqt[:, cols].T * scale).astype(bf16)
    local_out = [pltpu.make_async_copy(dq_out, dq_ref, lsem.at[6])]
    local_out[0].start()

    row_at = (row + ctx * TOK).astype(f32)
    angle = row_at * inv_ref[...]
    cosine, sine = jnp.cos(angle), jnp.sin(angle)

    total = summed(0)
    for s in range(REACH):
        arrived(n_bz + s, rz.at[0])
        total = total + rz[s].astype(f32)
    key_sum = total[:, 0:HEAD]
    value_half = total[:, HEAD:].astype(bf16)
    turned = pltpu.roll(key_sum, HEAD // 2, axis=1)
    turned = jnp.where(lane < HEAD // 2, -turned, turned)
    gloc[:, 0:HEAD] = (key_sum * cosine - turned * sine).astype(bf16)
    gloc[:, HEAD:] = value_half

    n_gy, n_g, n_o = sems.take(ny), sems.take(len(members)), sems.take(len(members))

    def tokens_of(d):
        return gloc.at[pl.ds(pl.multiple_of(lax.rem(y + d, ny) * piece, piece), piece)]

    for d in range(1, ny):
        send(n_gy + d, tokens_of(d), gy.at[y], at_y(d))
    gy[y] = gloc[pl.ds(pl.multiple_of(y * piece, piece), piece), :]
    dk_out[0] = key_sum.astype(bf16)
    dv_out[0] = value_half
    local_out.append(pltpu.make_async_copy(dk_out, dk_ref, lsem.at[7]))
    local_out.append(pltpu.make_async_copy(dv_out, dv_ref, lsem.at[8]))
    local_out[1].start()
    local_out[2].start()
    w_step(half - 1)
    for d in range(1, ny):
        arrived(n_gy + d, gy.at[0])

    for n, (dp, dx) in enumerate(members):
        send(n_g + n, gy, gall.at[me], at_member(dp, dx))
    gall[me] = gy[...]
    w_step(half)
    if nc == 2:
        arrived(n_over, wf.at[0, 0])
        for d in range(1, half + 1):
            low, high = ring_refs(d)
            arrived(n_over + 2 * d, low)
            arrived(n_over + 2 * d + 1, high)
    for n in range(len(members)):
        arrived(n_g + n, gy)

    count = 2 * nx
    tokens = jnp.concatenate(
        [gall[:, h].reshape(count * piece, 2 * HEAD) for h in range(ny)], axis=1
    )
    side = lax.rem(x, 2)
    whole = pl.ds(pl.multiple_of(side * (HEAD // 2), HEAD // 2), HEAD)
    rest = pl.ds(pl.multiple_of((1 - side) * HEAD, HEAD // 2), HEAD // 2)

    def weight_rows(n, rows):
        core, j = n // slots, n % slots
        return jnp.concatenate([wf[h, core, j, rows, :] for h in range(ny)], axis=1)

    shares = nc * slots
    for n in range(0, shares, 2):
        block = jnp.concatenate([weight_rows(n, whole), weight_rows(n + 1, whole)], axis=0)
        part = dot(tokens, block, NT).astype(bf16)
        obuf[:, :, n * HEAD : (n + 2) * HEAD] = part.reshape(count, piece, 2 * HEAD)
    for n in range(0, shares, 4):
        block = []
        for m in (n, n + 2):
            core, j = m // slots, m % slots
            first = jnp.concatenate([wf[h, core, j + side, rest, :] for h in range(ny)], axis=1)
            second = jnp.concatenate(
                [wf[h, core, j + 1 - side, rest, :] for h in range(ny)], axis=1
            )
            block += [first, second]
        part = dot(tokens, jnp.concatenate(block, axis=0), NT).astype(bf16)
        base = shares * HEAD + n * (HEAD // 2)
        obuf[:, :, base : base + 2 * HEAD] = part.reshape(count, piece, 2 * HEAD)

    for n, (dp, dx) in enumerate(members):
        send(n_o + n, obuf.at[member(dp, dx)], oin.at[me], at_member(dp, dx))
    oin[me] = obuf[me]
    for n in range(len(members)):
        arrived(n_o + n, oin.at[0])
    left = lax.broadcasted_iota(jnp.int32, (piece, HEAD), 1) < HEAD // 2
    for p in range(2):
        for e in range(nx // 2):
            even, uneven = p * nx + 2 * e, p * nx + 2 * e + 1
            for n in range(shares):
                core, j = n // slots, n % slots
                first = core * (nz * nx * rb) + (2 * j + p) * nx * rb + e * 2 * rb
                dx_out[0, :, first : first + HEAD] = oin[even, :, n * HEAD : (n + 1) * HEAD]
                dx_out[0, :, first + 2 * HEAD : first + 3 * HEAD] = oin[
                    uneven, :, n * HEAD : (n + 1) * HEAD
                ]
                base = shares * HEAD + n // 2 * HEAD
                a = oin[even, :, base : base + HEAD].astype(f32)
                b = oin[uneven, :, base : base + HEAD].astype(f32)
                if n % 2 == 0:
                    middle = jnp.where(left, a, b)
                else:
                    middle = pltpu.roll(jnp.where(left, b, a), HEAD // 2, axis=1)
                dx_out[0, :, first + HEAD : first + 2 * HEAD] = middle.astype(bf16)
    local_out.append(pltpu.make_async_copy(dx_out, dx_ref, lsem.at[9]))
    local_out[3].start()

    for s in range(planes):
        for d in range(nx - 1):
            sent(n_kx + s * (nx - 1) + d, kbuf.at[0, x])
            sent(n_vx + s * (nx - 1) + d, vbuf.at[0, mine])
            sent(n_bx + s * (nx - 1) + d, rx.at[0, 0])
        if s > 0:
            sent(n_kz + s, kbuf.at[0, x])
            sent(n_vz + s, vbuf.at[0, mine])
            sent(n_bz + s - 1, rz.at[0])
    for n, _ in wz:
        sent(n, w_ref)
    for d in range(1, half + 1):
        low, high = ring_refs(d)
        sent(n_up + d, low)
        sent(n_down + d, high)
        if nc == 2:
            sent(n_over + 2 * d, low)
            sent(n_over + 2 * d + 1, high)
    if nc == 2:
        sent(n_over, wf.at[0, 0])
    for d in range(1, ny):
        sent(n_gy + d, gy.at[0])
    for n in range(len(members)):
        sent(n_g + n, gy)
        sent(n_o + n, oin.at[0])
    for copy in local_out:
        copy.wait()


def hand_out(*refs):
    count = len(refs) // 2
    copies = [
        pltpu.make_async_copy(refs[n], refs[count + n], refs[-1].at[n]) for n in range(count)
    ]
    for copy in copies:
        copy.start()
    for copy in copies:
        copy.wait()


def local(sizes, q, k, v, o, do, lab, w):
    nc, nz, nx, ny = sizes
    group = q.shape[-1] // HEAD
    rb = w.shape[0]
    planes, keys, piece = REACH + 1, nx * TOK, TOK // ny
    d_all = rb * nc * nz * nx
    half = HEAD // 2
    inv = np.exp(
        -np.log(np.float32(1000000.0)) * (np.float32(2.0) * np.arange(half, dtype=np.float32) / HEAD)
    ).astype(np.float32)
    inv = jnp.asarray(np.concatenate([inv, inv])[None, :])
    copies = 160
    vm = pltpu.VMEM
    wide = group * TOK
    share = nc * (nz // 2) * rb
    scratch = [
        vm((TOK, wide), bf16),
        vm((TOK, wide), bf16),
        vm((TOK, wide), bf16),
        vm((wide, HEAD), bf16),
        vm((wide, 2 * HEAD), bf16),
        vm((planes, nx, PACK, HEAD), bf16),
        vm((planes, keys, HEAD), bf16),
        vm((HEAD, keys), bf16),
        vm((planes, keys, wide), f32),
        vm((keys, TOK), f32),
        vm((planes, 1, wide), f32),
        vm((planes, 1, wide), f32),
        vm((planes, 1, wide), f32),
        vm((HEAD, wide), f32),
        vm((keys, 2 * HEAD), f32),
        vm((planes, nx, TOK, 2 * HEAD), bf16),
        vm((planes, TOK, 2 * HEAD), f32),
        vm((planes, nx - 1, TOK, 2 * HEAD), bf16),
        vm((REACH, TOK, 2 * HEAD), bf16),
        vm((REACH, TOK, 2 * HEAD), bf16),
        vm((TOK, 2 * HEAD), bf16),
        vm((ny, piece, 2 * HEAD), bf16),
        vm((2 * nx, ny, piece, 2 * HEAD), bf16),
        vm((2 * nx, piece, share), bf16),
        vm((2 * nx, piece, share), bf16),
        vm((ny, nc, nz // 2, rb, 2 * HEAD), bf16),
        vm(q.shape, bf16),
        vm(k.shape, bf16),
        vm(v.shape, bf16),
        vm((1, piece, d_all), bf16),
        pltpu.SemaphoreType.DMA((copies,)),
        pltpu.SemaphoreType.DMA((copies,)),
        pltpu.SemaphoreType.DMA((10,)),
    ]
    spec = pl.BlockSpec(memory_space=pltpu.VMEM)
    far = pl.BlockSpec(memory_space=pltpu.HBM)
    results = tuple(
        jax.ShapeDtypeStruct(shape, bf16)
        for shape in (q.shape, k.shape, v.shape, (1, piece, d_all))
    )
    out = pl.pallas_call(
        functools.partial(kernel, nc, nz, nx, ny, group, rb),
        out_shape=results,
        in_specs=[spec] * 2 + [far] * 6,
        out_specs=(far,) * 4,
        scratch_shapes=scratch,
        compiler_params=pltpu.CompilerParams(
            collective_id=0, has_side_effects=True, vmem_limit_bytes=60 * 1024 * 1024
        ),
    )(lab, inv, q, k, v, o, do, w)
    return pl.pallas_call(
        hand_out,
        out_shape=results,
        in_specs=[far] * 4,
        out_specs=(far,) * 4,
        scratch_shapes=[pltpu.SemaphoreType.DMA((4,))],
    )(*out)


def solution(mesh):
    nx = NX
    sizes = (mesh.shape["dp"], mesh.shape["ctx"] // nx, nx, mesh.shape["tp"])
    in_specs = (
        P("dp", "ctx", "tp"),
        P("dp", "ctx", "tp"),
        P("dp", "ctx", "tp"),
        P("dp", "ctx", "tp"),
        P("dp", "ctx", "tp"),
        P("dp", "ctx"),
        P(("dp", "ctx"), "tp"),
    )
    out_specs = (
        P("dp", "ctx", "tp"),
        P("dp", "ctx", "tp"),
        P("dp", "ctx", "tp"),
        P("dp", ("ctx", "tp"), None),
    )
    return jax.shard_map(
        functools.partial(local, sizes),
        mesh=mesh, in_specs=in_specs, out_specs=out_specs, check_vma=False,
    )
```

time: 103 us -> 126 us (1.22)
  Pallas kernels: 97.8 us -> 125 us
  local copies, waits for them, and re-layouts: 3.96 us -> 0 us
    pallas_call x0 -> x1, Pallas kernels: none -> 26.9 us  [local(): pl.pallas_call(hand_out, out_shape=results, in_specs=[far] * 4, out_specs...]
    unnamed x10 -> x0, local copies, waits for them, and re-layouts: 3.96 us -> none
where the time goes in v2:
time: 126 us; the launch traced here: 125 us
  Pallas kernels  125 us (99%)
    pallas_call x1, Pallas kernels, local(): pl.pallas_call(functools.partial(kernel, nc, nz, nx, ny, group, rb), out_...  97.8 us
    pallas_call x1, Pallas kernels, local(): pl.pallas_call(hand_out, out_shape=results, in_specs=[far] * 4, out_specs...  26.9 us

profile of v2, /device:TPU:56, one launch (start us, length us, event | category | flops | bytes accessed | tf_op | source)
XLA Modules:
  0.0 125.3 jit_solution(17622533998744792737)
XLA Ops:
  0.6 97.8 %shard_map.111 = (bf16[1,128,1536]{2,1,0:T(8,128)(2,1)}, bf16[1,128,128]{2,1,0:T(8,128)(2,1)}, bf16[1,128,128]{2,1,0:T(8,128)(2,1)}, bf16[1,16,12288]{2,1,0:T(8,128)(2,1)}) custom-call(s32[1,128]{1,0:T(1,128)} %lab_ref.1, f32[1,128]{1,0:T(1,128)} %constant.2.clone.inv_ref, bf16[1,128,1536]{2,1,0:T(8,128)(2,1)} %q_ref.1, bf16[1,128,128]{2,1,0:T(8,128)(2,1)} %k_ref.1, ...), custom_call_target="tpu_custom_call" | custom-call | tf_op jit(solution)/shard_map/pallas_call | solution.py:499
  98.4 26.9 %shard_map.112 = (bf16[1,128,1536]{2,1,0:T(8,128)(2,1)}, bf16[1,128,128]{2,1,0:T(8,128)(2,1)}, bf16[1,128,128]{2,1,0:T(8,128)(2,1)}, bf16[1,16,12288]{2,1,0:T(8,128)(2,1)}) custom-call(bf16[1,128,1536]{2,1,0:T(8,128)(2,1)} %get-tuple-element.8.refs_0_, bf16[1,128,128]{2,1,0:T(8,128)(2,1)} %get-tuple-element.9.refs_1_, ...), custom_call_target="tpu_custom_call" | custom-call | tf_op jit(solution)/shard_map/pallas_call | solution.py:509

commit v3 on v2

--- a/solution.py
+++ b/solution.py
@@ -40,7 +40,7 @@
     lab_ref, inv_ref, q_ref, k_ref, v_ref, o_ref, do_ref, w_ref,
     dq_ref, dk_ref, dv_ref, dx_ref,
     qin, oin0, doin, qs, dos, kbuf, vbuf, kt, sbuf, bias, mrow, lrow, frow, dqt, acc,
-    outbox, own32, rx, zout, rz, gloc, gy, gall, obuf, oin, wf,
+    outbox, own32, rx, zout, rz, gloc, gy, gall, obuf, oin, wf, krelay, vrelay,
     dq_out, dk_out, dv_out, dx_out, ssem, rsem, lsem,
 ):
     c = lax.axis_index("dp")
@@ -98,7 +98,6 @@
         pl.semaphore_signal(barrier, inc=1, device_id=peer, device_id_type=MESH)
 
     mine = pl.ds(pl.multiple_of(x * TOK, TOK), TOK)
-    zslot = lax.div(z, 2)
     local_in = [
         pltpu.make_async_copy(src, dst, lsem.at[n])
         for n, (src, dst) in enumerate([
@@ -107,7 +106,7 @@
             (do_ref.at[0], doin),
             (o_ref.at[0], oin0),
             (q_ref.at[0], qin),
-            (w_ref, wf.at[y, c, zslot]),
+            (w_ref, wf.at[y, c, lax.div(z, 2)]),
         ])
     ]
     for copy in local_in:
@@ -129,15 +128,64 @@
         for d in range(1, nx):
             send(n_vx + s * (nx - 1) + d - 1, vbuf.at[s, mine], vbuf.at[s, mine], at(0, d))
 
+    n_kr, n_vr = sems.take(1), sems.take(1)
     keys_x(0)
-    for s in range(1, planes):
+    for s in range(1, REACH):
         send(n_kz + s, kbuf.at[0, x], kbuf.at[s, x], at(s, 0))
-    wz = [(sems.take(1), d) for d in range(2, nz, 2)]
-    for n, d in wz:
-        send(n, w_ref, wf.at[y, c, zslot], at(d, 0))
-    values_x(0)
-    for s in range(1, planes):
-        send(n_vz + s, vbuf.at[0, mine], vbuf.at[s, mine], at(s, 0))
+    send(n_kr, kbuf.at[0, x], krelay, at(-2, 0))
+
+    far = [0, 2, -2, 4]
+    n_w = sems.take(4)
+    n_up, n_down = sems.take(4 * (half + 1)), sems.take(4 * (half + 1))
+    n_over = sems.take(4 * (2 * half + 1))
+
+    def share(head, k):
+        return wf.at[head, c, lax.div(lax.rem(z + far[k] + nz, nz), 2)]
+
+    def low(d):
+        return lax.rem(y - d + ny, ny)
+
+    def high(d):
+        return lax.rem(y + d, ny)
+
+    def over(k, d, up):
+        return n_over + k * (2 * half + 1) + 2 * d - up
+
+    def goes_up(k, d):
+        return d < half or (d == half and k < 2)
+
+    def goes_down(k, d):
+        return d < half or (d == half and k >= 2)
+
+    def w_start(k, source=None):
+        source = share(y, k) if source is None else source
+        send(n_up + k * (half + 1) + 1, source, share(y, k), at_y(1))
+        send(n_down + k * (half + 1) + 1, source, share(y, k), at_y(-1))
+        if nc == 2:
+            send(over(k, 0, 0), source, share(y, k), sibling)
+
+    passed = set()
+
+    def w_pass(k, d):
+        if (k, d) in passed:
+            return
+        passed.add((k, d))
+        if goes_up(k, d):
+            arrived(n_up + k * (half + 1) + d, share(low(d), k))
+            if goes_up(k, d + 1):
+                send(n_up + k * (half + 1) + d + 1, share(low(d), k), share(low(d), k), at_y(1))
+            if nc == 2:
+                send(over(k, d, 1), share(low(d), k), share(low(d), k), sibling)
+        if goes_down(k, d):
+            arrived(n_down + k * (half + 1) + d, share(high(d), k))
+            if goes_down(k, d + 1):
+                send(n_down + k * (half + 1) + d + 1, share(high(d), k), share(high(d), k), at_y(-1))
+            if nc == 2:
+                send(over(k, d, 0), share(high(d), k), share(high(d), k), sibling)
+
+    send(n_w + 2, w_ref, share(y, 0), at(2, 0))
+    send(n_w + 1, w_ref, share(y, 0), at(-2, 0))
+    w_start(0, w_ref)
 
     for copy in local_in[2:]:
         copy.wait()
@@ -151,46 +199,22 @@
         delta = -jnp.sum(
             grad.astype(f32) * oin0[:, cols].astype(f32), axis=1, keepdims=True
         )
-        high = delta.astype(bf16).astype(f32)
-        middle = (delta - high).astype(bf16).astype(f32)
-        low = delta - high - middle
-        extra = jnp.where(lane == 0, high, jnp.where(lane == 1, middle, low))
+        first = delta.astype(bf16).astype(f32)
+        second = (delta - first).astype(bf16).astype(f32)
+        third = delta - first - second
+        extra = jnp.where(lane == 0, first, jnp.where(lane == 1, second, third))
         dos[part, HEAD:] = jnp.where(lane < 3, extra, 0.0).astype(bf16)
 
     dqt[...] = jnp.zeros_like(dqt)
     row = lax.broadcasted_iota(jnp.int32, (TOK, TOK), 0)
     query_at = lane + ctx * TOK
 
-    n_up, n_down, n_over = sems.take(half + 1), sems.take(half + 1), sems.take(2 * half + 2)
-    split = slots // 2
-
-    def ring_refs(d):
-        low, high = lax.rem(y - d + ny, ny), lax.rem(y + d, ny)
-        if d < half:
-            return wf.at[low, c], wf.at[high, c]
-        return wf.at[low, c, 0:split], wf.at[high, c, split:slots]
-
-    def w_begin():
-        for n, _ in wz:
-            arrived(n, wf.at[y, c, 0])
-        send(n_up + 1, wf.at[y, c], wf.at[y, c], at_y(1))
-        send(n_down + 1, wf.at[y, c], wf.at[y, c], at_y(-1))
-        if nc == 2:
-            send(n_over, wf.at[y, c], wf.at[y, c], sibling)
-
-    def w_step(d):
-        low, high = ring_refs(d)
-        arrived(n_up + d, low)
-        if d < half:
-            part = low if d + 1 < half else wf.at[lax.rem(y - d + ny, ny), c, 0:split]
-            send(n_up + d + 1, part, part, at_y(1))
-        arrived(n_down + d, high)
-        if d < half:
-            part = high if d + 1 < half else wf.at[lax.rem(y + d, ny), c, split:slots]
-            send(n_down + d + 1, part, part, at_y(-1))
-        if nc == 2:
-            send(n_over + 2 * d, low, low, sibling)
-            send(n_over + 2 * d + 1, high, high, sibling)
+    arrived(n_kr, krelay)
+    send(n_kz + REACH, krelay, kbuf.at[REACH, x], at(-2, 0))
+    values_x(0)
+    for s in range(1, REACH):
+        send(n_vz + s, vbuf.at[0, mine], vbuf.at[s, mine], at(s, 0))
+    send(n_vr, vbuf.at[0, mine], vrelay, at(-2, 0))
 
     def pass_one(s, carry):
         @pl.when(s < REACH)
@@ -198,10 +222,29 @@
             arrived(n_kz + s + 1, kbuf.at[0, x])
             keys_x(s + 1)
 
-        @pl.when(s > 0)
-        def _():
-            arrived(n_vz + s, vbuf.at[0, mine])
-            values_x(s)
+        @pl.when(s > 1)
+        def _():
+            arrived(n_vz + s - 1, vbuf.at[0, mine])
+            values_x(s - 1)
+
+        @pl.when(s == 1)
+        def _():
+            w_pass(0, 1)
+            arrived(n_w + 1, w_ref)
+            send(n_w + 3, share(y, 1), share(y, 1), at(-2, 0))
+            w_start(1)
+            arrived(n_w + 2, w_ref)
+            w_start(2)
+
+        @pl.when(s == 2)
+        def _():
+            arrived(n_vr, vrelay)
+            send(n_vz + REACH, vrelay, vbuf.at[REACH, mine], at(-2, 0))
+
+        @pl.when(s == REACH)
+        def _():
+            arrived(n_w + 3, w_ref)
+            w_start(3)
 
         for d in range(nx - 1):
             arrived(n_kx + s * (nx - 1) + d, kbuf.at[0, x])
@@ -225,13 +268,15 @@
             mrow[s, :, part] = top
             lrow[s, :, part] = jnp.sum(e, axis=0, keepdims=True)
 
-        @pl.when(s == 1)
-        def _():
-            w_begin()
-
         return carry
 
     lax.fori_loop(0, planes, pass_one, 0)
+
+    arrived(n_vz + REACH, vbuf.at[0, mine])
+    values_x(REACH)
+    w_pass(0, 2)
+    w_pass(1, 1)
+    w_pass(2, 1)
 
     top = mrow[0]
     for s in range(1, planes):
@@ -256,8 +301,16 @@
             total = total + rx[s, d].astype(f32)
         return total
 
+    def plane_at(r):
+        first = (REACH + 1 - r) // 3
+        return first * (r + 2) + (1 - first) * (REACH - r)
+
+    def back(s):
+        zout[s] = summed(s).astype(bf16)
+        send(n_bz + s, zout.at[s], rz.at[s], at(-s, 0))
+
     def pass_two(r, carry):
-        s = REACH - r
+        s = plane_at(r)
         for d in range(nx - 1):
             arrived(n_vx + s * (nx - 1) + d, vbuf.at[0, mine])
         block = jnp.concatenate([kbuf[s, other, 0:TOK] for other in range(nx)], axis=0)
@@ -277,19 +330,29 @@
                 outbox.at[s, lax.rem(x + d, nx)], rx.at[s, d - 1], at(0, d),
             )
 
-        @pl.when(s < REACH)
-        def _():
-            zout[s] = summed(s + 1).astype(bf16)
-            send(n_bz + s, zout.at[s], rz.at[s], at(-(s + 1), 0))
-
-        for d in range(1, half - 1):
-            @pl.when(s == half - 2 - d)
-            def _(d=d):
-                w_step(d)
+        @pl.when(r >= 2)
+        def _():
+            back(plane_at(r - 2))
+
+        @pl.when(r == 1)
+        def _():
+            w_pass(3, 1)
+
+        @pl.when(r == 3)
+        def _():
+            w_pass(0, 3)
+            w_pass(1, 2)
+            w_pass(2, 2)
+
+        @pl.when(r == REACH)
+        def _():
+            w_pass(3, 2)
 
         return carry
 
     lax.fori_loop(0, planes, pass_two, 0)
+
+    back(1)
 
     for h in range(group):
         cols = slice(h * HEAD, (h + 1) * HEAD)
@@ -302,7 +365,7 @@
     cosine, sine = jnp.cos(angle), jnp.sin(angle)
 
     total = summed(0)
-    for s in range(REACH):
+    for s in range(1, planes):
         arrived(n_bz + s, rz.at[0])
         total = total + rz[s].astype(f32)
     key_sum = total[:, 0:HEAD]
@@ -326,20 +389,24 @@
     local_out.append(pltpu.make_async_copy(dv_out, dv_ref, lsem.at[8]))
     local_out[1].start()
     local_out[2].start()
-    w_step(half - 1)
+    for k in range(4):
+        w_pass(k, 4 if k == 0 else 3)
     for d in range(1, ny):
         arrived(n_gy + d, gy.at[0])
 
     for n, (dp, dx) in enumerate(members):
         send(n_g + n, gy, gall.at[me], at_member(dp, dx))
     gall[me] = gy[...]
-    w_step(half)
+    for k in range(1, 4):
+        w_pass(k, half)
     if nc == 2:
-        arrived(n_over, wf.at[0, 0])
-        for d in range(1, half + 1):
-            low, high = ring_refs(d)
-            arrived(n_over + 2 * d, low)
-            arrived(n_over + 2 * d + 1, high)
+        for k in range(4):
+            arrived(over(k, 0, 0), w_ref)
+            for d in range(1, half + 1):
+                if goes_up(k, d):
+                    arrived(over(k, d, 1), w_ref)
+                if goes_down(k, d):
+                    arrived(over(k, d, 0), w_ref)
     for n in range(len(members)):
         arrived(n_g + n, gy)
 
@@ -408,18 +475,23 @@
         if s > 0:
             sent(n_kz + s, kbuf.at[0, x])
             sent(n_vz + s, vbuf.at[0, mine])
-            sent(n_bz + s - 1, rz.at[0])
-    for n, _ in wz:
-        sent(n, w_ref)
-    for d in range(1, half + 1):
-        low, high = ring_refs(d)
-        sent(n_up + d, low)
-        sent(n_down + d, high)
+            sent(n_bz + s, rz.at[0])
+    sent(n_kr, krelay)
+    sent(n_vr, vrelay)
+    for k in range(4):
+        if k > 0:
+            sent(n_w + k, w_ref)
+        for d in range(1, half + 1):
+            if goes_up(k, d):
+                sent(n_up + k * (half + 1) + d, w_ref)
+            if goes_down(k, d):
+                sent(n_down + k * (half + 1) + d, w_ref)
+            if nc == 2 and goes_up(k, d):
+                sent(over(k, d, 1), w_ref)
+            if nc == 2 and goes_down(k, d):
+                sent(over(k, d, 0), w_ref)
         if nc == 2:
-            sent(n_over + 2 * d, low)
-            sent(n_over + 2 * d + 1, high)
-    if nc == 2:
-        sent(n_over, wf.at[0, 0])
+            sent(over(k, 0, 0), w_ref)
     for d in range(1, ny):
         sent(n_gy + d, gy.at[0])
     for n in range(len(members)):
@@ -430,13 +502,16 @@
 
 
 def hand_out(*refs):
-    count = len(refs) // 2
-    copies = [
-        pltpu.make_async_copy(refs[n], refs[count + n], refs[-1].at[n]) for n in range(count)
-    ]
-    for copy in copies:
+    count = len(refs) // 3
+    sources, targets, held, sem = refs[:count], refs[count : 2 * count], refs[2 * count : -1], refs[-1]
+    into = [pltpu.make_async_copy(sources[n], held[n], sem.at[n]) for n in range(count)]
+    out = [pltpu.make_async_copy(held[n], targets[n], sem.at[count + n]) for n in range(count)]
+    for copy in into:
         copy.start()
-    for copy in copies:
+    for n in range(count):
+        into[n].wait()
+        out[n].start()
+    for copy in out:
         copy.wait()
 
 
@@ -451,7 +526,7 @@
         -np.log(np.float32(1000000.0)) * (np.float32(2.0) * np.arange(half, dtype=np.float32) / HEAD)
     ).astype(np.float32)
     inv = jnp.asarray(np.concatenate([inv, inv])[None, :])
-    copies = 160
+    copies = 200
     vm = pltpu.VMEM
     wide = group * TOK
     share = nc * (nz // 2) * rb
@@ -474,14 +549,16 @@
         vm((planes, nx, TOK, 2 * HEAD), bf16),
         vm((planes, TOK, 2 * HEAD), f32),
         vm((planes, nx - 1, TOK, 2 * HEAD), bf16),
-        vm((REACH, TOK, 2 * HEAD), bf16),
-        vm((REACH, TOK, 2 * HEAD), bf16),
+        vm((planes, TOK, 2 * HEAD), bf16),
+        vm((planes, TOK, 2 * HEAD), bf16),
         vm((TOK, 2 * HEAD), bf16),
         vm((ny, piece, 2 * HEAD), bf16),
         vm((2 * nx, ny, piece, 2 * HEAD), bf16),
         vm((2 * nx, piece, share), bf16),
         vm((2 * nx, piece, share), bf16),
         vm((ny, nc, nz // 2, rb, 2 * HEAD), bf16),
+        vm((PACK, HEAD), bf16),
+        vm((TOK, HEAD), bf16),
         vm(q.shape, bf16),
         vm(k.shape, bf16),
         vm(v.shape, bf16),
@@ -511,7 +588,7 @@
         out_shape=results,
         in_specs=[far] * 4,
         out_specs=(far,) * 4,
-        scratch_shapes=[pltpu.SemaphoreType.DMA((4,))],
+        scratch_shapes=[vm(r.shape, bf16) for r in results] + [pltpu.SemaphoreType.DMA((8,))],
     )(*out)
 
 

time: 126 us -> 81.8 us (0.65)
  the two profiles are of different devices: /device:TPU:56 before, /device:TPU:2 now
where the time goes in v3:
time: 81.8 us; the launch traced here: 81.7 us
  Pallas kernels  81 us (99%)
    pallas_call x1, Pallas kernels, local(): pl.pallas_call(functools.partial(kernel, nc, nz, nx, ny, group, rb), out_...  79 us
    pallas_call x1, Pallas kernels, local(): pl.pallas_call(hand_out, out_shape=results, in_specs=[far] * 4, out_specs...  1.97 us

profile of v3, /device:TPU:2, one launch (start us, length us, event | category | flops | bytes accessed | tf_op | source)
XLA Modules:
  0.0 81.7 jit_solution(2037578218767315551)
XLA Ops:
  0.6 79.0 %shard_map.111 = (bf16[1,128,1536]{2,1,0:T(8,128)(2,1)}, bf16[1,128,128]{2,1,0:T(8,128)(2,1)}, bf16[1,128,128]{2,1,0:T(8,128)(2,1)}, bf16[1,16,12288]{2,1,0:T(8,128)(2,1)}) custom-call(s32[1,128]{1,0:T(1,128)} %lab_ref.1, f32[1,128]{1,0:T(1,128)} %constant.2.clone.inv_ref, bf16[1,128,1536]{2,1,0:T(8,128)(2,1)} %q_ref.1, bf16[1,128,128]{2,1,0:T(8,128)(2,1)} %k_ref.1, ...), custom_call_target="tpu_custom_call" | custom-call | tf_op jit(solution)/shard_map/pallas_call | solution.py:576
  79.7 2.0 %shard_map.112 = (bf16[1,128,1536]{2,1,0:T(8,128)(2,1)}, bf16[1,128,128]{2,1,0:T(8,128)(2,1)}, bf16[1,128,128]{2,1,0:T(8,128)(2,1)}, bf16[1,16,12288]{2,1,0:T(8,128)(2,1)}) custom-call(bf16[1,128,1536]{2,1,0:T(8,128)(2,1)} %get-tuple-element.8.refs_0_, bf16[1,128,128]{2,1,0:T(8,128)(2,1)} %get-tuple-element.9.refs_1_, ...), custom_call_target="tpu_custom_call" | custom-call | tf_op jit(solution)/shard_map/pallas_call | solution.py:586

commit v4 on v3

--- a/solution.py
+++ b/solution.py
@@ -93,6 +93,10 @@
     peers = [at(d, 0) for d in range(1, nz)] + [at(0, d) for d in range(1, nx)]
     peers += [at_member(1, dx) for dx in range(1, nx)]
     peers += [at_y(d) for d in range(1, ny)] + ([sibling] if nc == 2 else [])
+    for s in (0, REACH):
+        kbuf[s] = jnp.zeros((nx, PACK, HEAD), bf16)
+        vbuf[s] = jnp.zeros((keys, HEAD), bf16)
+        rx[s] = jnp.zeros((nx - 1, TOK, 2 * HEAD), bf16)
     barrier = pltpu.get_barrier_semaphore()
     for peer in peers:
         pl.semaphore_signal(barrier, inc=1, device_id=peer, device_id_type=MESH)
@@ -103,9 +107,9 @@
         for n, (src, dst) in enumerate([
             (k_ref.at[0], kbuf.at[0, x, 0:TOK]),
             (v_ref.at[0], vbuf.at[0, mine]),
+            (q_ref.at[0], qin),
             (do_ref.at[0], doin),
             (o_ref.at[0], oin0),
-            (q_ref.at[0], qin),
             (w_ref, wf.at[y, c, lax.div(z, 2)]),
         ])
     ]
@@ -120,19 +124,33 @@
     n_kz, n_vz = sems.take(planes), sems.take(planes)
     n_kx, n_vx = sems.take(planes * (nx - 1)), sems.take(planes * (nx - 1))
 
+    def seen(s, key_x, query_x):
+        inside = (s > 0) & (s < REACH)
+        return inside | ((s == 0) & (key_x < query_x)) | ((s == REACH) & (key_x > query_x))
+
+    def from_x(d):
+        return lax.rem(x - d + nx, nx)
+
+    def to_x(d):
+        return lax.rem(x + d, nx)
+
     def keys_x(s):
         for d in range(1, nx):
-            send(n_kx + s * (nx - 1) + d - 1, kbuf.at[s, x], kbuf.at[s, x], at(0, d))
+            @pl.when(seen(s, x, to_x(d)))
+            def _(d=d):
+                send(n_kx + s * (nx - 1) + d - 1, kbuf.at[s, x], kbuf.at[s, x], at(0, d))
 
     def values_x(s):
         for d in range(1, nx):
-            send(n_vx + s * (nx - 1) + d - 1, vbuf.at[s, mine], vbuf.at[s, mine], at(0, d))
+            @pl.when(seen(s, x, to_x(d)))
+            def _(d=d):
+                send(n_vx + s * (nx - 1) + d - 1, vbuf.at[s, mine], vbuf.at[s, mine], at(0, d))
 
     n_kr, n_vr = sems.take(1), sems.take(1)
-    keys_x(0)
+    send(n_kr, kbuf.at[0, x], krelay, at(-2, 0))
     for s in range(1, REACH):
         send(n_kz + s, kbuf.at[0, x], kbuf.at[s, x], at(s, 0))
-    send(n_kr, kbuf.at[0, x], krelay, at(-2, 0))
+    keys_x(0)
 
     far = [0, 2, -2, 4]
     n_w = sems.take(4)
@@ -183,17 +201,30 @@
             if nc == 2:
                 send(over(k, d, 0), share(high(d), k), share(high(d), k), sibling)
 
+    w_start(0, w_ref)
+
+    local_in[2].wait()
+    for h in range(group):
+        qs[h * TOK : (h + 1) * TOK, :] = qin[:, h * HEAD : (h + 1) * HEAD]
+
+    arrived(n_kr, krelay)
+    send(n_kz + REACH, krelay, kbuf.at[REACH, x], at(-2, 0))
+    for s in (2, 3, 1):
+        send(n_vz + s, vbuf.at[0, mine], vbuf.at[s, mine], at(s, 0))
+    send(n_vr, vbuf.at[0, mine], vrelay, at(-2, 0))
+    for s in range(1, REACH):
+        arrived(n_kz + s, kbuf.at[0, x])
+        keys_x(s)
+    values_x(0)
     send(n_w + 2, w_ref, share(y, 0), at(2, 0))
     send(n_w + 1, w_ref, share(y, 0), at(-2, 0))
-    w_start(0, w_ref)
-
-    for copy in local_in[2:]:
+
+    for copy in local_in[3:]:
         copy.wait()
     lane = lax.broadcasted_iota(jnp.int32, (TOK, HEAD), 1)
     for h in range(group):
         cols = slice(h * HEAD, (h + 1) * HEAD)
         part = slice(h * TOK, (h + 1) * TOK)
-        qs[part, :] = qin[:, cols]
         grad = doin[:, cols]
         dos[part, 0:HEAD] = grad
         delta = -jnp.sum(
@@ -209,45 +240,34 @@
     row = lax.broadcasted_iota(jnp.int32, (TOK, TOK), 0)
     query_at = lane + ctx * TOK
 
-    arrived(n_kr, krelay)
-    send(n_kz + REACH, krelay, kbuf.at[REACH, x], at(-2, 0))
-    values_x(0)
-    for s in range(1, REACH):
-        send(n_vz + s, vbuf.at[0, mine], vbuf.at[s, mine], at(s, 0))
-    send(n_vr, vbuf.at[0, mine], vrelay, at(-2, 0))
-
     def pass_one(s, carry):
-        @pl.when(s < REACH)
-        def _():
-            arrived(n_kz + s + 1, kbuf.at[0, x])
-            keys_x(s + 1)
-
-        @pl.when(s > 1)
-        def _():
-            arrived(n_vz + s - 1, vbuf.at[0, mine])
-            values_x(s - 1)
-
         @pl.when(s == 1)
         def _():
+            arrived(n_kz + REACH, kbuf.at[0, x])
+            keys_x(REACH)
+            arrived(n_vr, vrelay)
+            send(n_vz + REACH, vrelay, vbuf.at[REACH, mine], at(-2, 0))
             w_pass(0, 1)
+
+        @pl.when(s == 2)
+        def _():
+            for n in (2, 3):
+                arrived(n_vz + n, vbuf.at[0, mine])
+                values_x(n)
+
+        @pl.when(s == REACH)
+        def _():
+            for n in (REACH, 1):
+                arrived(n_vz + n, vbuf.at[0, mine])
+                values_x(n)
             arrived(n_w + 1, w_ref)
             send(n_w + 3, share(y, 1), share(y, 1), at(-2, 0))
-            w_start(1)
-            arrived(n_w + 2, w_ref)
-            w_start(2)
-
-        @pl.when(s == 2)
-        def _():
-            arrived(n_vr, vrelay)
-            send(n_vz + REACH, vrelay, vbuf.at[REACH, mine], at(-2, 0))
-
-        @pl.when(s == REACH)
-        def _():
-            arrived(n_w + 3, w_ref)
-            w_start(3)
-
-        for d in range(nx - 1):
-            arrived(n_kx + s * (nx - 1) + d, kbuf.at[0, x])
+
+        for d in range(1, nx):
+            @pl.when(seen(s, from_x(d), x))
+            def _(d=d):
+                arrived(n_kx + s * (nx - 1) + d - 1, kbuf.at[0, x])
+
         plane = lax.rem(z - s + nz, nz)
         for other in range(nx):
             labels = kbuf[s, other, TOK:PACK].astype(f32)[0:1]
@@ -272,11 +292,10 @@
 
     lax.fori_loop(0, planes, pass_one, 0)
 
-    arrived(n_vz + REACH, vbuf.at[0, mine])
-    values_x(REACH)
     w_pass(0, 2)
-    w_pass(1, 1)
-    w_pass(2, 1)
+    w_start(1)
+    arrived(n_w + 2, w_ref)
+    w_start(2)
 
     top = mrow[0]
     for s in range(1, planes):
@@ -294,8 +313,11 @@
     n_bx, n_bz = sems.take(planes * (nx - 1)), sems.take(planes)
 
     def summed(s):
-        for d in range(nx - 1):
-            arrived(n_bx + s * (nx - 1) + d, rx.at[0, 0])
+        for d in range(1, nx):
+            @pl.when(seen(s, x, from_x(d)))
+            def _(d=d):
+                arrived(n_bx + s * (nx - 1) + d - 1, rx.at[0, 0])
+
         total = own32[s]
         for d in range(nx - 1):
             total = total + rx[s, d].astype(f32)
@@ -311,8 +333,11 @@
 
     def pass_two(r, carry):
         s = plane_at(r)
-        for d in range(nx - 1):
-            arrived(n_vx + s * (nx - 1) + d, vbuf.at[0, mine])
+        for d in range(1, nx):
+            @pl.when(seen(s, from_x(d), x))
+            def _(d=d):
+                arrived(n_vx + s * (nx - 1) + d - 1, vbuf.at[0, mine])
+
         block = jnp.concatenate([kbuf[s, other, 0:TOK] for other in range(nx)], axis=0)
         kt[...] = block.astype(f32).T.astype(bf16)
         prob = sbuf[s] * frow[s]
@@ -325,10 +350,12 @@
             outbox[s, other] = acc[other * TOK : (other + 1) * TOK, :].astype(bf16)
         own32[s] = acc[mine, :]
         for d in range(1, nx):
-            send(
-                n_bx + s * (nx - 1) + d - 1,
-                outbox.at[s, lax.rem(x + d, nx)], rx.at[s, d - 1], at(0, d),
-            )
+            @pl.when(seen(s, to_x(d), x))
+            def _(d=d):
+                send(
+                    n_bx + s * (nx - 1) + d - 1,
+                    outbox.at[s, to_x(d)], rx.at[s, d - 1], at(0, d),
+                )
 
         @pl.when(r >= 2)
         def _():
@@ -336,17 +363,20 @@
 
         @pl.when(r == 1)
         def _():
+            arrived(n_w + 3, w_ref)
+            w_start(3)
+
+        @pl.when(r == 2)
+        def _():
+            w_pass(1, 1)
+            w_pass(2, 1)
+            w_pass(0, 3)
+
+        @pl.when(r == REACH)
+        def _():
             w_pass(3, 1)
-
-        @pl.when(r == 3)
-        def _():
-            w_pass(0, 3)
             w_pass(1, 2)
             w_pass(2, 2)
-
-        @pl.when(r == REACH)
-        def _():
-            w_pass(3, 2)
 
         return carry
 
@@ -375,7 +405,7 @@
     gloc[:, 0:HEAD] = (key_sum * cosine - turned * sine).astype(bf16)
     gloc[:, HEAD:] = value_half
 
-    n_gy, n_g, n_o = sems.take(ny), sems.take(len(members)), sems.take(len(members))
+    n_gy, n_g, n_o = sems.take(ny), sems.take(len(members)), sems.take(2 * len(members))
 
     def tokens_of(d):
         return gloc.at[pl.ds(pl.multiple_of(lax.rem(y + d, ny) * piece, piece), piece)]
@@ -389,14 +419,15 @@
     local_out.append(pltpu.make_async_copy(dv_out, dv_ref, lsem.at[8]))
     local_out[1].start()
     local_out[2].start()
-    for k in range(4):
-        w_pass(k, 4 if k == 0 else 3)
+    for k, d in ((0, 4), (3, 2), (1, 3), (2, 3)):
+        w_pass(k, d)
     for d in range(1, ny):
         arrived(n_gy + d, gy.at[0])
 
     for n, (dp, dx) in enumerate(members):
         send(n_g + n, gy, gall.at[me], at_member(dp, dx))
     gall[me] = gy[...]
+    w_pass(3, 3)
     for k in range(1, 4):
         w_pass(k, half)
     if nc == 2:
@@ -427,6 +458,17 @@
         block = jnp.concatenate([weight_rows(n, whole), weight_rows(n + 1, whole)], axis=0)
         part = dot(tokens, block, NT).astype(bf16)
         obuf[:, :, n * HEAD : (n + 2) * HEAD] = part.reshape(count, piece, 2 * HEAD)
+    front = shares * HEAD
+    lots = (pl.ds(0, front), pl.ds(front, front // 2))
+
+    def hand_over(lot):
+        for n, (dp, dx) in enumerate(members):
+            send(
+                n_o + 2 * n + lot, obuf.at[member(dp, dx), :, lots[lot]],
+                oin.at[me, :, lots[lot]], at_member(dp, dx),
+            )
+
+    hand_over(0)
     for n in range(0, shares, 4):
         block = []
         for m in (n, n + 2):
@@ -437,14 +479,14 @@
             )
             block += [first, second]
         part = dot(tokens, jnp.concatenate(block, axis=0), NT).astype(bf16)
-        base = shares * HEAD + n * (HEAD // 2)
+        base = front + n * (HEAD // 2)
         obuf[:, :, base : base + 2 * HEAD] = part.reshape(count, piece, 2 * HEAD)
 
-    for n, (dp, dx) in enumerate(members):
-        send(n_o + n, obuf.at[member(dp, dx)], oin.at[me], at_member(dp, dx))
+    hand_over(1)
     oin[me] = obuf[me]
     for n in range(len(members)):
-        arrived(n_o + n, oin.at[0])
+        arrived(n_o + 2 * n, oin.at[0, :, lots[0]])
+        arrived(n_o + 2 * n + 1, oin.at[0, :, lots[1]])
     left = lax.broadcasted_iota(jnp.int32, (piece, HEAD), 1) < HEAD // 2
     for p in range(2):
         for e in range(nx // 2):
@@ -456,7 +498,7 @@
                 dx_out[0, :, first + 2 * HEAD : first + 3 * HEAD] = oin[
                     uneven, :, n * HEAD : (n + 1) * HEAD
                 ]
-                base = shares * HEAD + n // 2 * HEAD
+                base = front + n // 2 * HEAD
                 a = oin[even, :, base : base + HEAD].astype(f32)
                 b = oin[uneven, :, base : base + HEAD].astype(f32)
                 if n % 2 == 0:
@@ -468,10 +510,16 @@
     local_out[3].start()
 
     for s in range(planes):
-        for d in range(nx - 1):
-            sent(n_kx + s * (nx - 1) + d, kbuf.at[0, x])
-            sent(n_vx + s * (nx - 1) + d, vbuf.at[0, mine])
-            sent(n_bx + s * (nx - 1) + d, rx.at[0, 0])
+        for d in range(1, nx):
+            @pl.when(seen(s, x, to_x(d)))
+            def _(s=s, d=d):
+                sent(n_kx + s * (nx - 1) + d - 1, kbuf.at[0, x])
+                sent(n_vx + s * (nx - 1) + d - 1, vbuf.at[0, mine])
+
+            @pl.when(seen(s, to_x(d), x))
+            def _(s=s, d=d):
+                sent(n_bx + s * (nx - 1) + d - 1, rx.at[0, 0])
+
         if s > 0:
             sent(n_kz + s, kbuf.at[0, x])
             sent(n_vz + s, vbuf.at[0, mine])
@@ -496,7 +544,8 @@
         sent(n_gy + d, gy.at[0])
     for n in range(len(members)):
         sent(n_g + n, gy)
-        sent(n_o + n, oin.at[0])
+        sent(n_o + 2 * n, oin.at[0, :, lots[0]])
+        sent(n_o + 2 * n + 1, oin.at[0, :, lots[1]])
     for copy in local_out:
         copy.wait()
 

time: 81.8 us -> 78.5 us (0.960)
  the two profiles are of different devices: /device:TPU:2 before, /device:TPU:56 now
where the time goes in v4:
time: 78.5 us; the launch traced here: 76.9 us
  Pallas kernels  76.3 us (97%)
    pallas_call x1, Pallas kernels, local(): pl.pallas_call(functools.partial(kernel, nc, nz, nx, ny, group, rb), out_...  74.3 us
    pallas_call x1, Pallas kernels, local(): pl.pallas_call(hand_out, out_shape=results, in_specs=[far] * 4, out_specs...  1.97 us

profile of v4, /device:TPU:56, one launch (start us, length us, event | category | flops | bytes accessed | tf_op | source)
XLA Modules:
  0.0 76.9 jit_solution(13287504980198610907)
XLA Ops:
  0.6 74.3 %shard_map.111 = (bf16[1,128,1536]{2,1,0:T(8,128)(2,1)}, bf16[1,128,128]{2,1,0:T(8,128)(2,1)}, bf16[1,128,128]{2,1,0:T(8,128)(2,1)}, bf16[1,16,12288]{2,1,0:T(8,128)(2,1)}) custom-call(s32[1,128]{1,0:T(1,128)} %lab_ref.1, f32[1,128]{1,0:T(1,128)} %constant.2.clone.inv_ref, bf16[1,128,1536]{2,1,0:T(8,128)(2,1)} %q_ref.1, bf16[1,128,128]{2,1,0:T(8,128)(2,1)} %k_ref.1, ...), custom_call_target="tpu_custom_call" | custom-call | tf_op jit(solution)/shard_map/pallas_call | solution.py:625
  75.0 2.0 %shard_map.112 = (bf16[1,128,1536]{2,1,0:T(8,128)(2,1)}, bf16[1,128,128]{2,1,0:T(8,128)(2,1)}, bf16[1,128,128]{2,1,0:T(8,128)(2,1)}, bf16[1,16,12288]{2,1,0:T(8,128)(2,1)}) custom-call(bf16[1,128,1536]{2,1,0:T(8,128)(2,1)} %get-tuple-element.8.refs_0_, bf16[1,128,128]{2,1,0:T(8,128)(2,1)} %get-tuple-element.9.refs_1_, ...), custom_call_target="tpu_custom_call" | custom-call | tf_op jit(solution)/shard_map/pallas_call | solution.py:635

commit v5 on v4

--- a/solution.py
+++ b/solution.py
@@ -96,7 +96,6 @@
     for s in (0, REACH):
         kbuf[s] = jnp.zeros((nx, PACK, HEAD), bf16)
         vbuf[s] = jnp.zeros((keys, HEAD), bf16)
-        rx[s] = jnp.zeros((nx - 1, TOK, 2 * HEAD), bf16)
     barrier = pltpu.get_barrier_semaphore()
     for peer in peers:
         pl.semaphore_signal(barrier, inc=1, device_id=peer, device_id_type=MESH)
@@ -207,18 +206,6 @@
     for h in range(group):
         qs[h * TOK : (h + 1) * TOK, :] = qin[:, h * HEAD : (h + 1) * HEAD]
 
-    arrived(n_kr, krelay)
-    send(n_kz + REACH, krelay, kbuf.at[REACH, x], at(-2, 0))
-    for s in (2, 3, 1):
-        send(n_vz + s, vbuf.at[0, mine], vbuf.at[s, mine], at(s, 0))
-    send(n_vr, vbuf.at[0, mine], vrelay, at(-2, 0))
-    for s in range(1, REACH):
-        arrived(n_kz + s, kbuf.at[0, x])
-        keys_x(s)
-    values_x(0)
-    send(n_w + 2, w_ref, share(y, 0), at(2, 0))
-    send(n_w + 1, w_ref, share(y, 0), at(-2, 0))
-
     for copy in local_in[3:]:
         copy.wait()
     lane = lax.broadcasted_iota(jnp.int32, (TOK, HEAD), 1)
@@ -239,6 +226,18 @@
     dqt[...] = jnp.zeros_like(dqt)
     row = lax.broadcasted_iota(jnp.int32, (TOK, TOK), 0)
     query_at = lane + ctx * TOK
+
+    arrived(n_kr, krelay)
+    send(n_kz + REACH, krelay, kbuf.at[REACH, x], at(-2, 0))
+    for s in (2, 3, 1):
+        send(n_vz + s, vbuf.at[0, mine], vbuf.at[s, mine], at(s, 0))
+    send(n_vr, vbuf.at[0, mine], vrelay, at(-2, 0))
+    for s in range(1, REACH):
+        arrived(n_kz + s, kbuf.at[0, x])
+        keys_x(s)
+    values_x(0)
+    send(n_w + 2, w_ref, share(y, 0), at(2, 0))
+    send(n_w + 1, w_ref, share(y, 0), at(-2, 0))
 
     def pass_one(s, carry):
         @pl.when(s == 1)
@@ -320,7 +319,8 @@
 
         total = own32[s]
         for d in range(nx - 1):
-            total = total + rx[s, d].astype(f32)
+            got = rx[s, d].astype(f32)
+            total = total + jnp.where(seen(s, x, from_x(d + 1)), got, 0.0)
         return total
 
     def plane_at(r):

time: 78.5 us -> 78.4 us (level)
  the two profiles are of different devices: /device:TPU:56 before, /device:TPU:25 now
where the time goes in v5:
time: 78.4 us; the launch traced here: 78.3 us
  Pallas kernels  77.6 us (99%)
    pallas_call x1, Pallas kernels, local(): pl.pallas_call(functools.partial(kernel, nc, nz, nx, ny, group, rb), out_...  75.7 us
    pallas_call x1, Pallas kernels, local(): pl.pallas_call(hand_out, out_shape=results, in_specs=[far] * 4, out_specs...  1.97 us

profile of v5, /device:TPU:25, one launch (start us, length us, event | category | flops | bytes accessed | tf_op | source)
XLA Modules:
  0.0 78.3 jit_solution(2745085240626326987)
XLA Ops:
  0.6 75.7 %shard_map.111 = (bf16[1,128,1536]{2,1,0:T(8,128)(2,1)}, bf16[1,128,128]{2,1,0:T(8,128)(2,1)}, bf16[1,128,128]{2,1,0:T(8,128)(2,1)}, bf16[1,16,12288]{2,1,0:T(8,128)(2,1)}) custom-call(s32[1,128]{1,0:T(1,128)} %lab_ref.1, f32[1,128]{1,0:T(1,128)} %constant.2.clone.inv_ref, bf16[1,128,1536]{2,1,0:T(8,128)(2,1)} %q_ref.1, bf16[1,128,128]{2,1,0:T(8,128)(2,1)} %k_ref.1, ...), custom_call_target="tpu_custom_call" | custom-call | tf_op jit(solution)/shard_map/pallas_call | solution.py:625
  76.3 2.0 %shard_map.112 = (bf16[1,128,1536]{2,1,0:T(8,128)(2,1)}, bf16[1,128,128]{2,1,0:T(8,128)(2,1)}, bf16[1,128,128]{2,1,0:T(8,128)(2,1)}, bf16[1,16,12288]{2,1,0:T(8,128)(2,1)}) custom-call(bf16[1,128,1536]{2,1,0:T(8,128)(2,1)} %get-tuple-element.8.refs_0_, bf16[1,128,128]{2,1,0:T(8,128)(2,1)} %get-tuple-element.9.refs_1_, ...), custom_call_target="tpu_custom_call" | custom-call | tf_op jit(solution)/shard_map/pallas_call | solution.py:635
